TPU v7x, 512 devices: a whole 4x8x8 slice. The times are simulated.
512 devices in a mesh: dp: 32 (over x, z), ctx: 16 (over y, core).
Axes of the slice: x: 4, y: 8, z: 8, core: 2. Of those that a mesh axis runs over, the one named last changes fastest.
Arguments:
- ssm_input: bfloat16 [65536, 4096], P(('dp', 'ctx')), parts along dimension 0, may hold values from -6 to 6
- gate_input: bfloat16 [65536, 4096], P(('dp', 'ctx')), parts along dimension 0, may hold values from -6 to 6
- b_proj: bfloat16 [65536, 512], P(('dp', 'ctx')), parts along dimension 0, may hold values from -0.1796875 to 0.1796875
- c_proj: bfloat16 [65536, 512], P(('dp', 'ctx')), parts along dimension 0, may hold values from -6 to 6
- dt_raw: float32 [65536, 64], P(('dp', 'ctx')), parts along dimension 0, may hold values from -3 to 3
- a_log: float32 [64], replicated, may hold values from -12 to -3
- skip: float32 [64], replicated, may hold values from 1 to 3
- norm_gain: float32 [4096], replicated, may hold values from 0.5 to 1.5
- queries: bfloat16 [65536, 2048], P(('dp', 'ctx')), parts along dimension 0, may hold values from -110 to 110
- keys: bfloat16 [65536, 512], P(('dp', 'ctx')), parts along dimension 0, may hold values from -5 to 5
- values: bfloat16 [65536, 512], P(('dp', 'ctx')), parts along dimension 0, may hold values from -6 to 6
- block_lists: int32 [512, 3], P(('dp', 'ctx')), parts along dimension 0, may hold values from -1 to 14, as said below
Outputs:
- ssm_out: bfloat16 [65536, 4096], P(('dp', 'ctx')), parts along dimension 0
- attn_out: bfloat16 [65536, 2048], P(('dp', 'ctx')), parts along dimension 0
There are 32 independent parts, one for each index of `dp`. A program takes and returns all parts, laid end to end along the dimension named above; an argument that names none is the same for every part. Nothing has to cross between parts.
Inputs may be any that keep to these rules, and one draw needn't show every extreme that they name: `block_lists`: row b lists distinct key blocks below b in its first slots and -1 in the others; every row b >= 1 lists at least one; the last row fills all 3 slots and lists 16 - 2; row 0 lists none.
All inputs are finite; a program needn't handle non-finite values.
Results may differ from a plain program's by a relative error of at most 0.015.
Values may be sent and summed in bfloat16 or wider, within the bound.
A program may use at most 192 MiB of HBM per device.

v0:
```python
import jax
import jax.numpy as jnp
from jax import lax
from jax.sharding import PartitionSpec as P

SSM_HEADS = 64
HEAD_P = 64
STATE = 128
GROUPS = 4
QHEADS = 16
KVHEADS = 4
HEAD_D = 128
BLK = 128


NORM_EPS = 1e-05
FAR_BELOW = -1e30


def prefix(shard, axis, combine, identity):
    peers, place = (lax.axis_size(axis), lax.axis_index(axis))
    everything = jax.tree.map(
        lambda part, kind: lax.all_gather(part.astype(kind), axis),
        shard,
        (jnp.bfloat16, jnp.bfloat16),
    )
    start = jax.tree.map(
        lambda part, zero: jnp.broadcast_to(jnp.asarray(zero, part.dtype), part.shape),
        shard,
        identity,
    )

    def step(k, before):
        reached = k < place
        new = combine(
            before, jax.tree.map(lambda part, own: part[k].astype(own.dtype), everything, shard)
        )
        return jax.tree.map(lambda a, b: jnp.where(reached, a, b), new, before)

    return lax.fori_loop(0, peers, step, start)


def from_behind(value, axis, steps):
    count = lax.axis_size(axis)
    first, last = (max(0, -steps), min(count, count - steps))
    return lax.ppermute(value, axis, [(source, source + steps) for source in range(first, last)])


def block_terms(inputs_blk, steps_blk, b_blk, c_blk, head_rates):
    running = jnp.cumsum(-steps_blk * head_rates, axis=0)
    scaled = (inputs_blk.astype(jnp.float32) * steps_blk[..., None]).astype(jnp.bfloat16)
    products = jnp.einsum("tgn,sgn->gts", c_blk, b_blk, preferred_element_type=jnp.float32)
    ordered = jnp.transpose(running, (1, 2, 0))
    spacing = ordered[..., :, None] - ordered[..., None, :]
    length = running.shape[0]
    lower_tri = jnp.arange(length)[:, None] >= jnp.arange(length)[None, :]
    decays = jnp.where(lower_tri, jnp.exp(jnp.where(lower_tri, spacing, 0.0)), 0.0)
    mixing = (decays * products[:, None]).astype(jnp.bfloat16)
    diag_out = jnp.einsum("gjts,sgjp->tgjp", mixing, scaled, preferred_element_type=jnp.float32)
    tail_decay = jnp.exp(running[-1] - running)
    b_decay = (b_blk.astype(jnp.float32)[:, :, None, :] * tail_decay[..., None]).astype(
        jnp.bfloat16
    )
    span_state = jnp.einsum("sgjp,sgjn->gjpn", scaled, b_decay, preferred_element_type=jnp.float32)
    return (diag_out, span_state, running)


def finish(mixed, ssm_input, gate_input, skip, norm_gain):
    layout = mixed.shape
    with_skip = mixed + skip.reshape(layout[1], layout[2], 1) * ssm_input.reshape(layout).astype(
        jnp.float32
    )
    gated = with_skip * jax.nn.silu(gate_input.astype(jnp.float32)).reshape(layout)
    grouped = gated.reshape(layout[0], layout[1], layout[2] * layout[3])
    scale_rms = lax.rsqrt(jnp.mean(grouped * grouped, axis=-1, keepdims=True) + NORM_EPS)
    normed = grouped * scale_rms * norm_gain.reshape(1, layout[1], -1)
    return normed.reshape(layout[0], -1).astype(jnp.bfloat16)


def body(
    ssm_input,
    gate_input,
    b_proj,
    c_proj,
    dt_raw,
    a_log,
    skip,
    norm_gain,
    queries,
    keys,
    values,
    block_lists,
):
    tok_rows = ssm_input.shape[0]
    per_group = SSM_HEADS // GROUPS
    blocks = tok_rows // BLK
    inputs_all = ssm_input.reshape(blocks, BLK, GROUPS, per_group, HEAD_P)
    steps_all = jax.nn.softplus(dt_raw).reshape(blocks, BLK, GROUPS, per_group)
    b_all = b_proj.reshape(blocks, BLK, GROUPS, STATE)
    c_all = c_proj.reshape(blocks, BLK, GROUPS, STATE)
    head_rates = jnp.exp(a_log).reshape(GROUPS, per_group)

    def advance(state, pieces):
        inputs_blk, steps_blk, b_blk, c_blk = pieces
        diag_out, span_state, running = block_terms(inputs_blk, steps_blk, b_blk, c_blk, head_rates)
        after = jnp.exp(running[-1])[..., None, None] * state + span_state
        return (after, (diag_out, state, running))

    start_state = jnp.zeros((GROUPS, per_group, HEAD_P, STATE), jnp.float32)
    local_end, (diag_all, local_starts, running_all) = lax.scan(
        advance, start_state, (inputs_all, steps_all, b_all, c_all)
    )
    block_decay = jnp.exp(running_all[:, -1])
    device_decay = jnp.prod(block_decay, axis=0)

    def combine(earlier, later):
        return (earlier[0] * later[0], later[0][..., None, None] * earlier[1] + later[1])

    identity = (jnp.ones_like(device_decay), jnp.zeros_like(local_end))
    _, entering = prefix((device_decay, local_end), "ctx", combine, identity)
    leading = jnp.cumprod(
        jnp.concatenate([jnp.ones_like(block_decay), block_decay[:-1]], axis=0), axis=0
    )
    start_states = local_starts + leading[..., None, None] * entering[None]
    rounded = start_states.astype(jnp.bfloat16)
    from_state = jnp.einsum("ctgn,cgjpn->ctgjp", c_all, rounded, preferred_element_type=jnp.float32)
    mixed = diag_all + jnp.exp(running_all)[..., None] * from_state
    ssm_out = finish(
        mixed.reshape(tok_rows, GROUPS, per_group, HEAD_P), ssm_input, gate_input, skip, norm_gain
    )
    ratio_heads = QHEADS // KVHEADS
    my_index = lax.axis_index("ctx")
    query_heads = queries.reshape(tok_rows, KVHEADS, ratio_heads, HEAD_D)
    query_pos = my_index * tok_rows + jnp.arange(tok_rows, dtype=jnp.int32)
    query_block = query_pos // BLK
    row_lists = jnp.repeat(block_lists, BLK, axis=0)
    scale_score = HEAD_D ** (-0.5)

    def absorb(stats, kv_piece, first_row):
        key_piece, value_piece = kv_piece
        count_rows = key_piece.shape[0]
        key_pos = first_row + jnp.arange(count_rows, dtype=jnp.int32)
        key_block = key_pos // BLK
        listed = jnp.any(row_lists[:, :, None] == key_block[None, None, :], axis=1)
        visible = listed | (key_block[None, :] == query_block[:, None]) & (
            key_pos[None, :] <= query_pos[:, None]
        )
        key_heads = key_piece.reshape(count_rows, KVHEADS, HEAD_D)
        value_heads = value_piece.reshape(count_rows, KVHEADS, HEAD_D)

        def update(old_stats):
            top_old, sum_old, acc_old = old_stats
            scores = (
                jnp.einsum(
                    "tkgd,skd->kgts", query_heads, key_heads, preferred_element_type=jnp.float32
                )
                * scale_score
            )
            scores = jnp.where(visible, scores, -jnp.inf)
            top_new = jnp.maximum(top_old, jnp.max(scores, axis=-1))
            weight = jnp.exp(scores - top_new[..., None])
            fading = jnp.exp(top_old - top_new)
            sum_new = fading * sum_old + jnp.sum(weight, axis=-1)
            added = jnp.einsum(
                "kgts,skd->tkgd",
                weight.astype(jnp.bfloat16),
                value_heads,
                preferred_element_type=jnp.float32,
            )
            acc_new = acc_old * jnp.transpose(fading, (2, 0, 1))[..., None] + added
            return (top_new, sum_new, acc_new)

        def unchanged(old_stats):
            return old_stats

        return lax.cond(jnp.any(visible), update, unchanged, stats)

    init_stats = (
        jnp.full((KVHEADS, ratio_heads, tok_rows), FAR_BELOW, jnp.float32),
        jnp.zeros((KVHEADS, ratio_heads, tok_rows), jnp.float32),
        jnp.zeros((tok_rows, KVHEADS, ratio_heads, HEAD_D), jnp.float32),
    )
    stats = absorb(init_stats, (keys, values), my_index * tok_rows)

    def cycle_turn(turn_index, state_all):
        stats_now, packed = state_all
        packed = from_behind(packed, "ctx", 1)
        source = (my_index - turn_index) % lax.axis_size("ctx")
        return (absorb(stats_now, (packed[0], packed[1]), source * tok_rows), packed)

    stats, _ = lax.fori_loop(
        1, lax.axis_size("ctx"), cycle_turn, (stats, jnp.stack([keys, values]))
    )
    _, sum_final, acc_final = stats
    attn_out = acc_final / jnp.transpose(sum_final, (2, 0, 1))[..., None]
    return (ssm_out, attn_out.reshape(tok_rows, QHEADS * HEAD_D).astype(jnp.bfloat16))


def solution(mesh):
    in_specs = (
        P(("dp", "ctx"), None),
        P(("dp", "ctx"), None),
        P(("dp", "ctx"), None),
        P(("dp", "ctx"), None),
        P(("dp", "ctx"), None),
        P(),
        P(),
        P(),
        P(("dp", "ctx"), None),
        P(("dp", "ctx"), None),
        P(("dp", "ctx"), None),
        P(("dp", "ctx"), None),
    )
    out_specs = (P(("dp", "ctx"), None), P(("dp", "ctx"), None))
    return jax.shard_map(body, mesh=mesh, in_specs=in_specs, out_specs=out_specs, check_vma=False)
```

profile of v0, /device:TPU:69, one launch (start us, length us, event | category | flops | bytes accessed | tf_op | source)
XLA Modules:
  0.0 304.3 jit_solution(11451111909306376104)
XLA Ops:
  10.9 2.5 add_convert_fusion
  20.5 6.3 %conditional.2 = (f32[4,4,128]{2,1,0:T(4,128)}, f32[4,4,128]{2,1,0:T(4,128)S(1)}, f32[128,4,4,128]{3,0,2,1:T(8,128)S(1)}) conditional(s32[]{:T(128)} %convert_element_type.127, () %tuple.62, (pred[128,128]{1,0:T(8,128)(4,1)}, bf16[128,512]{1,0:T(8,128)(2,1)S(1)}, bf16[128,4,4,128]{0,3,2,1:T(8,128)(2,1)S(1)}, bf16[128,512]{1,0:T(8,128)(2,1)S(1)}) %tuple.145), branch_computations={%region_6.7_spmd, %region_7.10_spmd} | conditional | flops 136323072 | bytes 11935824 | solution.py:176
  28.6 175.2 %while.45 = (s32[]{:T(128)}, f32[4,4,128]{2,1,0:T(4,128)}, f32[4,4,128]{2,1,0:T(4,128)S(1)}, f32[128,4,4,128]{3,0,2,1:T(8,128)S(1)}, bf16[2,128,512]{1,2,0:T(8,1...) while((s32[]{:T(128)}, f32[4,4,128]{2,1,0:T(4,128)}, ...), condition=%wide.region_17.18_spmd.clone.clone, body=%wide.region_10.17_spmd.clone.clone.sunk | while | flops 136751120 | bytes 8492068 | solution.py:191
  28.6 3.8 %collective-permute-start = (bf16[2,128,512]{1,2,0:T(8,128)(2,1)}, bf16[2,128,512]{1,2,0:T(8,128)(2,1)S(1)}, u32[]{:S(2)}, u32[]{:S(2)}) collective-permute-start(bf16[2,128,512]{1,2,0:T(8,128)(2,1)} %get-tuple-element.775), channel_id=1, source_target_pairs={{0,1},{1,2},{2,3},{3,4},{4,5},{5,6},{6,7},{7,8},{8,9},{9,10},{10,1... | collective-permute-start | bytes 786440 | tf_op jit(solution)/shard_map/while/body/eval_jaxpr/ppermute | solution.py:46
  35.1 6.2 %collective-permute-done = bf16[2,128,512]{1,2,0:T(8,128)(2,1)S(1)} collective-permute-done((bf16[2,128,512]{1,2,0:T(8,128)(2,1)}, bf16[2,128,512]{1,2,0:T(8,128)(2,1)S(1)}, u32[]{:S(2)}, u32[]{:S(2)}) %collective-permute-start) | collective-permute-done | bytes 262176 | tf_op jit(solution)/shard_map/while/body/eval_jaxpr/ppermute | solution.py:46
  41.3 6.5 %conditional.6 = ((f32[4,4,128]{2,1,0:T(4,128)}, f32[4,4,128]{2,1,0:T(4,128)S(1)}, f32[128,4,4,128]{3,0,2,1:T(8,128)S(1)})) conditional(s32[]{:T(128)} %convert_element_type.174, (f32[4,4,128]{2,1,0:T(4,128)}, f32[4,4,128]{2,1,0:T(4,128)S(1)}, f32[128,4,4,128]{3,0,2,1:T(8,128)S(1)}) %tuple.126, (pred[128,128]{1,0:T(8,128)(4,1)}, ...), branch_computations={%region_13.13_spmd, %region_14.16_spmd} | conditional | flops 136583168 | bytes 6865040 | solution.py:176
  48.5 1.9 collective-permute-start
  53.2 6.4 %collective-permute-done = bf16[2,128,512]{1,2,0:T(8,128)(2,1)S(1)} collective-permute-done((bf16[2,128,512]{1,2,0:T(8,128)(2,1)}, bf16[2,128,512]{1,2,0:T(8,128)(2,1)S(1)}, u32[]{:S(2)}, u32[]{:S(2)}) %collective-permute-start) | collective-permute-done | bytes 262176 | tf_op jit(solution)/shard_map/while/body/eval_jaxpr/ppermute | solution.py:46
  60.3 10.7 %collective-permute-start = (bf16[2,128,512]{1,2,0:T(8,128)(2,1)}, bf16[2,128,512]{1,2,0:T(8,128)(2,1)S(1)}, u32[]{:S(2)}, u32[]{:S(2)}) collective-permute-start(bf16[2,128,512]{1,2,0:T(8,128)(2,1)} %get-tuple-element.775), channel_id=1, source_target_pairs={{0,1},{1,2},{2,3},{3,4},{4,5},{5,6},{6,7},{7,8},{8,9},{9,10},{10,1... | collective-permute-start | bytes 786440 | tf_op jit(solution)/shard_map/while/body/eval_jaxpr/ppermute | solution.py:46
  73.9 6.4 %collective-permute-done = bf16[2,128,512]{1,2,0:T(8,128)(2,1)S(1)} collective-permute-done((bf16[2,128,512]{1,2,0:T(8,128)(2,1)}, bf16[2,128,512]{1,2,0:T(8,128)(2,1)S(1)}, u32[]{:S(2)}, u32[]{:S(2)}) %collective-permute-start) | collective-permute-done | bytes 262176 | tf_op jit(solution)/shard_map/while/body/eval_jaxpr/ppermute | solution.py:46
  81.0 4.3 %collective-permute-start = (bf16[2,128,512]{1,2,0:T(8,128)(2,1)}, bf16[2,128,512]{1,2,0:T(8,128)(2,1)S(1)}, u32[]{:S(2)}, u32[]{:S(2)}) collective-permute-start(bf16[2,128,512]{1,2,0:T(8,128)(2,1)} %get-tuple-element.775), channel_id=1, source_target_pairs={{0,1},{1,2},{2,3},{3,4},{4,5},{5,6},{6,7},{7,8},{8,9},{9,10},{10,1... | collective-permute-start | bytes 786440 | tf_op jit(solution)/shard_map/while/body/eval_jaxpr/ppermute | solution.py:46
  88.1 6.4 %collective-permute-done = bf16[2,128,512]{1,2,0:T(8,128)(2,1)S(1)} collective-permute-done((bf16[2,128,512]{1,2,0:T(8,128)(2,1)}, bf16[2,128,512]{1,2,0:T(8,128)(2,1)S(1)}, u32[]{:S(2)}, u32[]{:S(2)}) %collective-permute-start) | collective-permute-done | bytes 262176 | tf_op jit(solution)/shard_map/while/body/eval_jaxpr/ppermute | solution.py:46
  95.2 4.3 %collective-permute-start = (bf16[2,128,512]{1,2,0:T(8,128)(2,1)}, bf16[2,128,512]{1,2,0:T(8,128)(2,1)S(1)}, u32[]{:S(2)}, u32[]{:S(2)}) collective-permute-start(bf16[2,128,512]{1,2,0:T(8,128)(2,1)} %get-tuple-element.775), channel_id=1, source_target_pairs={{0,1},{1,2},{2,3},{3,4},{4,5},{5,6},{6,7},{7,8},{8,9},{9,10},{10,1... | collective-permute-start | bytes 786440 | tf_op jit(solution)/shard_map/while/body/eval_jaxpr/ppermute | solution.py:46
  102.2 6.4 %collective-permute-done = bf16[2,128,512]{1,2,0:T(8,128)(2,1)S(1)} collective-permute-done((bf16[2,128,512]{1,2,0:T(8,128)(2,1)}, bf16[2,128,512]{1,2,0:T(8,128)(2,1)S(1)}, u32[]{:S(2)}, u32[]{:S(2)}) %collective-permute-start) | collective-permute-done | bytes 262176 | tf_op jit(solution)/shard_map/while/body/eval_jaxpr/ppermute | solution.py:46
  109.4 4.3 %collective-permute-start = (bf16[2,128,512]{1,2,0:T(8,128)(2,1)}, bf16[2,128,512]{1,2,0:T(8,128)(2,1)S(1)}, u32[]{:S(2)}, u32[]{:S(2)}) collective-permute-start(bf16[2,128,512]{1,2,0:T(8,128)(2,1)} %get-tuple-element.775), channel_id=1, source_target_pairs={{0,1},{1,2},{2,3},{3,4},{4,5},{5,6},{6,7},{7,8},{8,9},{9,10},{10,1... | collective-permute-start | bytes 786440 | tf_op jit(solution)/shard_map/while/body/eval_jaxpr/ppermute | solution.py:46
  116.4 6.4 %collective-permute-done = bf16[2,128,512]{1,2,0:T(8,128)(2,1)S(1)} collective-permute-done((bf16[2,128,512]{1,2,0:T(8,128)(2,1)}, bf16[2,128,512]{1,2,0:T(8,128)(2,1)S(1)}, u32[]{:S(2)}, u32[]{:S(2)}) %collective-permute-start) | collective-permute-done | bytes 262176 | tf_op jit(solution)/shard_map/while/body/eval_jaxpr/ppermute | solution.py:46
  123.6 5.4 %collective-permute-start = (bf16[2,128,512]{1,2,0:T(8,128)(2,1)}, bf16[2,128,512]{1,2,0:T(8,128)(2,1)S(1)}, u32[]{:S(2)}, u32[]{:S(2)}) collective-permute-start(bf16[2,128,512]{1,2,0:T(8,128)(2,1)} %get-tuple-element.775), channel_id=1, source_target_pairs={{0,1},{1,2},{2,3},{3,4},{4,5},{5,6},{6,7},{7,8},{8,9},{9,10},{10,1... | collective-permute-start | bytes 786440 | tf_op jit(solution)/shard_map/while/body/eval_jaxpr/ppermute | solution.py:46
  133.3 4.3 %collective-permute-start = (bf16[2,128,512]{1,2,0:T(8,128)(2,1)}, bf16[2,128,512]{1,2,0:T(8,128)(2,1)S(1)}, u32[]{:S(2)}, u32[]{:S(2)}) collective-permute-start(bf16[2,128,512]{1,2,0:T(8,128)(2,1)} %get-tuple-element.775), channel_id=1, source_target_pairs={{0,1},{1,2},{2,3},{3,4},{4,5},{5,6},{6,7},{7,8},{8,9},{9,10},{10,1... | collective-permute-start | bytes 786440 | tf_op jit(solution)/shard_map/while/body/eval_jaxpr/ppermute | solution.py:46
  141.9 4.3 %collective-permute-start = (bf16[2,128,512]{1,2,0:T(8,128)(2,1)}, bf16[2,128,512]{1,2,0:T(8,128)(2,1)S(1)}, u32[]{:S(2)}, u32[]{:S(2)}) collective-permute-start(bf16[2,128,512]{1,2,0:T(8,128)(2,1)} %get-tuple-element.775), channel_id=1, source_target_pairs={{0,1},{1,2},{2,3},{3,4},{4,5},{5,6},{6,7},{7,8},{8,9},{9,10},{10,1... | collective-permute-start | bytes 786440 | tf_op jit(solution)/shard_map/while/body/eval_jaxpr/ppermute | solution.py:46
  150.5 4.3 %collective-permute-start = (bf16[2,128,512]{1,2,0:T(8,128)(2,1)}, bf16[2,128,512]{1,2,0:T(8,128)(2,1)S(1)}, u32[]{:S(2)}, u32[]{:S(2)}) collective-permute-start(bf16[2,128,512]{1,2,0:T(8,128)(2,1)} %get-tuple-element.775), channel_id=1, source_target_pairs={{0,1},{1,2},{2,3},{3,4},{4,5},{5,6},{6,7},{7,8},{8,9},{9,10},{10,1... | collective-permute-start | bytes 786440 | tf_op jit(solution)/shard_map/while/body/eval_jaxpr/ppermute | solution.py:46
  159.1 4.3 %collective-permute-start = (bf16[2,128,512]{1,2,0:T(8,128)(2,1)}, bf16[2,128,512]{1,2,0:T(8,128)(2,1)S(1)}, u32[]{:S(2)}, u32[]{:S(2)}) collective-permute-start(bf16[2,128,512]{1,2,0:T(8,128)(2,1)} %get-tuple-element.775), channel_id=1, source_target_pairs={{0,1},{1,2},{2,3},{3,4},{4,5},{5,6},{6,7},{7,8},{8,9},{9,10},{10,1... | collective-permute-start | bytes 786440 | tf_op jit(solution)/shard_map/while/body/eval_jaxpr/ppermute | solution.py:46
  167.7 4.3 %collective-permute-start = (bf16[2,128,512]{1,2,0:T(8,128)(2,1)}, bf16[2,128,512]{1,2,0:T(8,128)(2,1)S(1)}, u32[]{:S(2)}, u32[]{:S(2)}) collective-permute-start(bf16[2,128,512]{1,2,0:T(8,128)(2,1)} %get-tuple-element.775), channel_id=1, source_target_pairs={{0,1},{1,2},{2,3},{3,4},{4,5},{5,6},{6,7},{7,8},{8,9},{9,10},{10,1... | collective-permute-start | bytes 786440 | tf_op jit(solution)/shard_map/while/body/eval_jaxpr/ppermute | solution.py:46
  176.4 4.3 %collective-permute-start = (bf16[2,128,512]{1,2,0:T(8,128)(2,1)}, bf16[2,128,512]{1,2,0:T(8,128)(2,1)S(1)}, u32[]{:S(2)}, u32[]{:S(2)}) collective-permute-start(bf16[2,128,512]{1,2,0:T(8,128)(2,1)} %get-tuple-element.775), channel_id=1, source_target_pairs={{0,1},{1,2},{2,3},{3,4},{4,5},{5,6},{6,7},{7,8},{8,9},{9,10},{10,1... | collective-permute-start | bytes 786440 | tf_op jit(solution)/shard_map/while/body/eval_jaxpr/ppermute | solution.py:46
  185.0 4.6 %collective-permute-start = (bf16[2,128,512]{1,2,0:T(8,128)(2,1)}, bf16[2,128,512]{1,2,0:T(8,128)(2,1)S(1)}, u32[]{:S(2)}, u32[]{:S(2)}) collective-permute-start(bf16[2,128,512]{1,2,0:T(8,128)(2,1)} %get-tuple-element.775), channel_id=1, source_target_pairs={{0,1},{1,2},{2,3},{3,4},{4,5},{5,6},{6,7},{7,8},{8,9},{9,10},{10,1... | collective-permute-start | bytes 786440 | tf_op jit(solution)/shard_map/while/body/eval_jaxpr/ppermute | solution.py:46
  193.9 5.5 %collective-permute-start = (bf16[2,128,512]{1,2,0:T(8,128)(2,1)}, bf16[2,128,512]{1,2,0:T(8,128)(2,1)S(1)}, u32[]{:S(2)}, u32[]{:S(2)}) collective-permute-start(bf16[2,128,512]{1,2,0:T(8,128)(2,1)} %get-tuple-element.775), channel_id=1, source_target_pairs={{0,1},{1,2},{2,3},{3,4},{4,5},{5,6},{6,7},{7,8},{8,9},{9,10},{10,1... | collective-permute-start | bytes 786440 | tf_op jit(solution)/shard_map/while/body/eval_jaxpr/ppermute | solution.py:46
  205.3 2.3 convert_element_type.129
  210.9 2.3 copy.93
  213.2 43.8 %all-gather = bf16[16,1,4,16]{3,2,1,0:T(4,128)(2,1)S(1)} all-gather(bf16[1,1,4,16]{3,2,1,0:T(4,128)(2,1)S(1)} %fusion.53), channel_id=2, replica_groups=mesh['dp'=32,'ctx'=16] {'ctx'}, dimensions={0}, use_global_device_ids=true | all-gather | bytes 2176 | tf_op jit(solution)/shard_map/all_gather | solution.py:23
  258.2 4.2 %fusion.26 = f32[4,16,64,128]{3,2,1,0:T(8,128)} fusion(f32[4,128,128]{2,1,0:T(8,128)S(1)} %fusion.46, f32[4,16,128]{2,1,0:T(8,128)} %copy.85, pred[128,128]{1,0:T(8,128)(4,1)S(1)} %iota_compare_fusion, f32[128,4,16]{0,2,1:T(8,128)} %bitcast.138, bf16[128,4,16,64]{0,3,2,1:T(8,128)(2,1)S(1)} %bitcast.117), kind=kOutput, calls=%fused_computation.49 | convolution fusion | flops 141033472 | bytes 3489792 | tf_op jit(solution)/shard_map/while/body/eval_jaxpr/gjts,sgjp->tgjp/dot_general | solution.py:59
  262.4 28.9 %while.44 = (s32[]{:T(128)}, f32[4,16,64,128]{3,2,1,0:T(8,128)S(1)}, s32[]{:T(128)}, bf16[16,4,16]{2,1,0:T(4,128)(2,1)S(1)}, bf16[16,4,16,64,128]{4,3,2,1,0:T(8,128)(2,1)}, /*index=5*/s32[]{:T(128)}, s32[]{:T(128)}) while((s32[]{:T(128)}, f32[4,16,64,128]{3,2,1,0:T(8,128)S(1)}, s32[]{:T(128)}, bf16[16,4,16]{2,1,0:T(4,128)(2,1)S(1)}, ...), condition=%wide.region_2.3_spmd.clone, body=%wide.region_1.2_spmd.clone.sunk | while | flops 2621508 | bytes 5243625 | solution.py:40
  264.2 1.8 fusion.71
  291.3 2.1 fusion.31
  (230 shorter events, 111.0 us)
Async XLA Ops:
  7.2 2.9 copy-start.7
  7.2 3.6 %copy-start.11 = (bf16[128,512]{1,0:T(8,128)(2,1)S(1)}, bf16[128,512]{1,0:T(8,128)(2,1)}, u32[]{:S(2)}) copy-start(bf16[128,512]{1,0:T(8,128)(2,1)} %param.22) | copy-start | bytes 393220
  7.2 255.2 %all-gather.4.cloned.1.call-start = ((), (), s32[]{:S(2)}) async-start(), calls=%async_computation | async-start | bytes 17825792 | tf_op jit(solution)/shard_map/all_gather | solution.py:23
  8.1 2.8 copy-start.17
  10.8 2.6 copy-start
  10.9 2.6 copy-start.21
  10.9 4.1 %copy-start.8 = (bf16[128,2048]{1,0:T(8,128)(2,1)S(1)}, bf16[128,2048]{1,0:T(8,128)(2,1)}, u32[]{:S(2)}) copy-start(bf16[128,2048]{1,0:T(8,128)(2,1)} %param.28) | copy-start | bytes 1572868
  13.4 2.9 copy-start.9
  13.4 3.6 %copy-start.10 = (bf16[128,512]{1,0:T(8,128)(2,1)S(1)}, bf16[128,512]{1,0:T(8,128)(2,1)}, u32[]{:S(2)}) copy-start(bf16[128,512]{1,0:T(8,128)(2,1)} %param.30) | copy-start | bytes 393220
  22.8 2.3 copy-start.3
  28.6 12.8 %collective-permute-start = (bf16[2,128,512]{1,2,0:T(8,128)(2,1)}, bf16[2,128,512]{1,2,0:T(8,128)(2,1)S(1)}, u32[]{:S(2)}, u32[]{:S(2)}) collective-permute-start(bf16[2,128,512]{1,2,0:T(8,128)(2,1)} %get-tuple-element.775), channel_id=1, source_target_pairs={{0,1},{1,2},{2,3},{3,4},{4,5},{5,6},{6,7},{7,8},{8,9},{9,10},{10,1... | collective-permute-start | bytes 786440 | tf_op jit(solution)/shard_map/while/body/eval_jaxpr/ppermute | solution.py:46
  42.8 2.4 copy-start.13
  46.5 1.3 copy-start.15
  48.5 11.1 %collective-permute-start = (bf16[2,128,512]{1,2,0:T(8,128)(2,1)}, bf16[2,128,512]{1,2,0:T(8,128)(2,1)S(1)}, u32[]{:S(2)}, u32[]{:S(2)}) collective-permute-start(bf16[2,128,512]{1,2,0:T(8,128)(2,1)} %get-tuple-element.775), channel_id=1, source_target_pairs={{0,1},{1,2},{2,3},{3,4},{4,5},{5,6},{6,7},{7,8},{8,9},{9,10},{10,1... | collective-permute-start | bytes 786440 | tf_op jit(solution)/shard_map/while/body/eval_jaxpr/ppermute | solution.py:46
  60.3 19.9 %collective-permute-start = (bf16[2,128,512]{1,2,0:T(8,128)(2,1)}, bf16[2,128,512]{1,2,0:T(8,128)(2,1)S(1)}, u32[]{:S(2)}, u32[]{:S(2)}) collective-permute-start(bf16[2,128,512]{1,2,0:T(8,128)(2,1)} %get-tuple-element.775), channel_id=1, source_target_pairs={{0,1},{1,2},{2,3},{3,4},{4,5},{5,6},{6,7},{7,8},{8,9},{9,10},{10,1... | collective-permute-start | bytes 786440 | tf_op jit(solution)/shard_map/while/body/eval_jaxpr/ppermute | solution.py:46
  81.0 13.5 %collective-permute-start = (bf16[2,128,512]{1,2,0:T(8,128)(2,1)}, bf16[2,128,512]{1,2,0:T(8,128)(2,1)S(1)}, u32[]{:S(2)}, u32[]{:S(2)}) collective-permute-start(bf16[2,128,512]{1,2,0:T(8,128)(2,1)} %get-tuple-element.775), channel_id=1, source_target_pairs={{0,1},{1,2},{2,3},{3,4},{4,5},{5,6},{6,7},{7,8},{8,9},{9,10},{10,1... | collective-permute-start | bytes 786440 | tf_op jit(solution)/shard_map/while/body/eval_jaxpr/ppermute | solution.py:46
  95.2 13.5 %collective-permute-start = (bf16[2,128,512]{1,2,0:T(8,128)(2,1)}, bf16[2,128,512]{1,2,0:T(8,128)(2,1)S(1)}, u32[]{:S(2)}, u32[]{:S(2)}) collective-permute-start(bf16[2,128,512]{1,2,0:T(8,128)(2,1)} %get-tuple-element.775), channel_id=1, source_target_pairs={{0,1},{1,2},{2,3},{3,4},{4,5},{5,6},{6,7},{7,8},{8,9},{9,10},{10,1... | collective-permute-start | bytes 786440 | tf_op jit(solution)/shard_map/while/body/eval_jaxpr/ppermute | solution.py:46
  109.4 13.5 %collective-permute-start = (bf16[2,128,512]{1,2,0:T(8,128)(2,1)}, bf16[2,128,512]{1,2,0:T(8,128)(2,1)S(1)}, u32[]{:S(2)}, u32[]{:S(2)}) collective-permute-start(bf16[2,128,512]{1,2,0:T(8,128)(2,1)} %get-tuple-element.775), channel_id=1, source_target_pairs={{0,1},{1,2},{2,3},{3,4},{4,5},{5,6},{6,7},{7,8},{8,9},{9,10},{10,1... | collective-permute-start | bytes 786440 | tf_op jit(solution)/shard_map/while/body/eval_jaxpr/ppermute | solution.py:46
  123.6 9.0 %collective-permute-start = (bf16[2,128,512]{1,2,0:T(8,128)(2,1)}, bf16[2,128,512]{1,2,0:T(8,128)(2,1)S(1)}, u32[]{:S(2)}, u32[]{:S(2)}) collective-permute-start(bf16[2,128,512]{1,2,0:T(8,128)(2,1)} %get-tuple-element.775), channel_id=1, source_target_pairs={{0,1},{1,2},{2,3},{3,4},{4,5},{5,6},{6,7},{7,8},{8,9},{9,10},{10,1... | collective-permute-start | bytes 786440 | tf_op jit(solution)/shard_map/while/body/eval_jaxpr/ppermute | solution.py:46
  133.3 7.9 %collective-permute-start = (bf16[2,128,512]{1,2,0:T(8,128)(2,1)}, bf16[2,128,512]{1,2,0:T(8,128)(2,1)S(1)}, u32[]{:S(2)}, u32[]{:S(2)}) collective-permute-start(bf16[2,128,512]{1,2,0:T(8,128)(2,1)} %get-tuple-element.775), channel_id=1, source_target_pairs={{0,1},{1,2},{2,3},{3,4},{4,5},{5,6},{6,7},{7,8},{8,9},{9,10},{10,1... | collective-permute-start | bytes 786440 | tf_op jit(solution)/shard_map/while/body/eval_jaxpr/ppermute | solution.py:46
  141.9 7.9 %collective-permute-start = (bf16[2,128,512]{1,2,0:T(8,128)(2,1)}, bf16[2,128,512]{1,2,0:T(8,128)(2,1)S(1)}, u32[]{:S(2)}, u32[]{:S(2)}) collective-permute-start(bf16[2,128,512]{1,2,0:T(8,128)(2,1)} %get-tuple-element.775), channel_id=1, source_target_pairs={{0,1},{1,2},{2,3},{3,4},{4,5},{5,6},{6,7},{7,8},{8,9},{9,10},{10,1... | collective-permute-start | bytes 786440 | tf_op jit(solution)/shard_map/while/body/eval_jaxpr/ppermute | solution.py:46
  150.5 7.9 %collective-permute-start = (bf16[2,128,512]{1,2,0:T(8,128)(2,1)}, bf16[2,128,512]{1,2,0:T(8,128)(2,1)S(1)}, u32[]{:S(2)}, u32[]{:S(2)}) collective-permute-start(bf16[2,128,512]{1,2,0:T(8,128)(2,1)} %get-tuple-element.775), channel_id=1, source_target_pairs={{0,1},{1,2},{2,3},{3,4},{4,5},{5,6},{6,7},{7,8},{8,9},{9,10},{10,1... | collective-permute-start | bytes 786440 | tf_op jit(solution)/shard_map/while/body/eval_jaxpr/ppermute | solution.py:46
  159.1 7.9 %collective-permute-start = (bf16[2,128,512]{1,2,0:T(8,128)(2,1)}, bf16[2,128,512]{1,2,0:T(8,128)(2,1)S(1)}, u32[]{:S(2)}, u32[]{:S(2)}) collective-permute-start(bf16[2,128,512]{1,2,0:T(8,128)(2,1)} %get-tuple-element.775), channel_id=1, source_target_pairs={{0,1},{1,2},{2,3},{3,4},{4,5},{5,6},{6,7},{7,8},{8,9},{9,10},{10,1... | collective-permute-start | bytes 786440 | tf_op jit(solution)/shard_map/while/body/eval_jaxpr/ppermute | solution.py:46
  167.7 7.9 %collective-permute-start = (bf16[2,128,512]{1,2,0:T(8,128)(2,1)}, bf16[2,128,512]{1,2,0:T(8,128)(2,1)S(1)}, u32[]{:S(2)}, u32[]{:S(2)}) collective-permute-start(bf16[2,128,512]{1,2,0:T(8,128)(2,1)} %get-tuple-element.775), channel_id=1, source_target_pairs={{0,1},{1,2},{2,3},{3,4},{4,5},{5,6},{6,7},{7,8},{8,9},{9,10},{10,1... | collective-permute-start | bytes 786440 | tf_op jit(solution)/shard_map/while/body/eval_jaxpr/ppermute | solution.py:46
  176.4 7.9 %collective-permute-start = (bf16[2,128,512]{1,2,0:T(8,128)(2,1)}, bf16[2,128,512]{1,2,0:T(8,128)(2,1)S(1)}, u32[]{:S(2)}, u32[]{:S(2)}) collective-permute-start(bf16[2,128,512]{1,2,0:T(8,128)(2,1)} %get-tuple-element.775), channel_id=1, source_target_pairs={{0,1},{1,2},{2,3},{3,4},{4,5},{5,6},{6,7},{7,8},{8,9},{9,10},{10,1... | collective-permute-start | bytes 786440 | tf_op jit(solution)/shard_map/while/body/eval_jaxpr/ppermute | solution.py:46
  185.0 8.3 %collective-permute-start = (bf16[2,128,512]{1,2,0:T(8,128)(2,1)}, bf16[2,128,512]{1,2,0:T(8,128)(2,1)S(1)}, u32[]{:S(2)}, u32[]{:S(2)}) collective-permute-start(bf16[2,128,512]{1,2,0:T(8,128)(2,1)} %get-tuple-element.775), channel_id=1, source_target_pairs={{0,1},{1,2},{2,3},{3,4},{4,5},{5,6},{6,7},{7,8},{8,9},{9,10},{10,1... | collective-permute-start | bytes 786440 | tf_op jit(solution)/shard_map/while/body/eval_jaxpr/ppermute | solution.py:46
  193.9 9.1 %collective-permute-start = (bf16[2,128,512]{1,2,0:T(8,128)(2,1)}, bf16[2,128,512]{1,2,0:T(8,128)(2,1)S(1)}, u32[]{:S(2)}, u32[]{:S(2)}) collective-permute-start(bf16[2,128,512]{1,2,0:T(8,128)(2,1)} %get-tuple-element.775), channel_id=1, source_target_pairs={{0,1},{1,2},{2,3},{3,4},{4,5},{5,6},{6,7},{7,8},{8,9},{9,10},{10,1... | collective-permute-start | bytes 786440 | tf_op jit(solution)/shard_map/while/body/eval_jaxpr/ppermute | solution.py:46
  203.7 5.5 %copy-start.6 = (f32[128,4,16]{2,1,0:T(4,128)S(1)}, f32[128,4,16]{2,1,0:T(4,128)}, u32[]{:S(2)}) copy-start(f32[128,4,16]{2,1,0:T(4,128)} %copy-done.5) | copy-start | bytes 98308
  205.3 52.9 %copy-start.1 = (bf16[128,4096]{0,1:T(8,128)(2,1)S(1)}, bf16[128,4096]{0,1:T(8,128)(2,1)}, u32[]{:S(2)}) copy-start(bf16[128,4096]{0,1:T(8,128)(2,1)} %copy-done) | copy-start | bytes 3145732
  262.4 28.9 %copy-start.16 = (f32[128,4,16]{0,2,1:T(8,128)S(1)}, f32[128,4,16]{0,2,1:T(8,128)}, u32[]{:S(2)}) copy-start(f32[128,4,16]{0,2,1:T(8,128)} %copy.89) | copy-start | bytes 98308
  291.3 2.1 copy-start.2
  291.3 2.1 copy-start.19
  (6 other events, 5.1 us)
Sparse Core Ops, SparseCore 0:
  13.5 113.4 all-gather.3
where the time goes:
time: 309 us; the launch traced here: 304 us
  other arithmetic  72.4 us (23%)
  starting transfers between devices  70.4 us (23%)
  waiting for transfers between devices  46 us (15%)
  blocking collectives  43.8 us (14%)
  local copies, waits for them, and re-layouts  30.8 us (10%)
  matrix products  15.2 us (5%)
  between operations  14.9 us (5%)
  loops' own time  10.6 us (3%)
    ppermute x15, starting transfers between devices, from_behind(): lax.ppermute(value, axis, [(source, source + steps) for source in range(f...  70.4 us
    ppermute x15, waiting for transfers between devices, from_behind(): lax.ppermute(value, axis, [(source, source + steps) for source in range(f...  46 us
    all_gather x1, blocking collectives, prefix(): lax.all_gather(part.astype(kind), axis)  43.8 us
    select_n x16, other arithmetic, step(): return jax.tree.map(lambda a, b: jnp.where(reached, a, b), new, before)  28.3 us
    reduce_or x16, other arithmetic, absorb(): return lax.cond(jnp.any(visible), update, unchanged, stats)  21.6 us
    reduce_or x16, other arithmetic, absorb(): listed = jnp.any(row_lists[:, :, None] == key_block[None, None, :], axis=1)  11.8 us
    while x15, local copies, waits for them, and re-layouts  10.7 us
    another operation x1, loops' own time, body(): lax.fori_loop(1, lax.axis_size('ctx'), cycle_turn, (stats, jnp.stack([key...  10.1 us
  transfers between devices with their start and end apart: 16, of which 15 were waited for; matrix products, arithmetic and copies ran while one was open for 25% of the time, Pallas kernels for 0%

commit v1 on v0

v1 whole, which is shorter than its diff:
```python
import jax
import jax.numpy as jnp
from jax import lax
from jax.experimental import pallas as pl
from jax.experimental.pallas import tpu as pltpu
from jax.sharding import PartitionSpec as P

MESH = pl.DeviceIdType.MESH
F32 = jnp.float32
BF16 = jnp.bfloat16

SSM_HEADS = 64
HEAD_P = 64
GROUPS = 4
KVHEADS = 4
RATIO = 4
HEAD_D = 128
BLK = 128
NORM_EPS = 1e-05
MASKED = -1e30

CHIPS = 8
HALF = 512
COLS = 1024
PIECE = 128
CHUNKS = 16
UP_STEPS = 3
DOWN_STEPS = 4
LAG_NUM, LAG_DEN = 9, 2
KV_TICKS = 4
ATTN_LAST = 34
ATTN_FIRST = 26
TICKS = 64


def dot(a, b):
    return lax.dot_general(a, b, (((1,), (0,)), ((), ())), preferred_element_type=F32)


def dot_t(a, b):
    return lax.dot_general(a, b, (((1,), (1,)), ((), ())), preferred_element_type=F32)


def split(v):
    hi = v.astype(BF16)
    return hi, (v - hi.astype(F32)).astype(BF16)


def kernel(
    x_hbm, gate_hbm, b_hbm, c_hbm, dt_hbm, alog_hbm, skip_hbm, gain_hbm, q_hbm, k_hbm, v_hbm, list_hbm,
    ssm_hbm, attn_hbm,
    x, gate, b, cp, dtr, alog, skip, gain, q, lists,
    kv, stack, xs, u, a1, a2, local, sib, dec, dsib, chip, isend, pin, enter, ssm_v, attn_v,
    in_sem, out_sem,
    up_s, up_r, down_s, down_r, kvsib_s, kvsib_r, chain_s, chain_r, psib_s, psib_r, ex_s, ex_r,
):
    me = lax.axis_index("ctx")
    y = lax.div(me, 2)
    c = lax.rem(me, 2)
    oc = 1 - c
    above = lax.rem(y + 1, CHIPS) * 2 + c
    below = lax.rem(y + CHIPS - 1, CHIPS) * 2 + c
    other = y * 2 + oc

    barrier = pltpu.get_barrier_semaphore()
    for peer in (above, below, other):
        pl.semaphore_signal(barrier, inc=1, device_id={"ctx": peer}, device_id_type=MESH)

    loads = [
        pltpu.make_async_copy(src, dst, in_sem.at[i])
        for i, (src, dst) in enumerate(
            (
                (dt_hbm, dtr), (alog_hbm, alog), (skip_hbm, skip), (b_hbm, b), (x_hbm, x),
                (k_hbm, kv.at[me, 0]), (v_hbm, kv.at[me, 1]), (c_hbm, cp), (gate_hbm, gate), (gain_hbm, gain),
                (q_hbm, q), (list_hbm, lists),
            )
        )
    ]
    for load in loads:
        load.start()

    def remote(src, dst, send, recv, to):
        return pltpu.make_async_remote_copy(
            src_ref=src, dst_ref=dst, send_sem=send, recv_sem=recv, device_id={"ctx": to}, device_id_type=MESH
        )

    def up_copy(e):
        slot = lax.rem(y - lax.div(e, 2) + CHIPS, CHIPS) * 2 + c
        part = lax.rem(e, 2)
        return remote(kv.at[slot, part], kv.at[slot, part], up_s.at[e], up_r.at[e], above)

    def up_arrival(e):
        slot = lax.rem(y - 1 - lax.div(e, 2) + CHIPS, CHIPS) * 2 + c
        part = lax.rem(e, 2)
        return remote(kv.at[slot, part], kv.at[slot, part], up_s.at[e], up_r.at[e], above), slot, part

    def down_copy(e):
        slot = lax.rem(y + lax.div(e, 2), CHIPS) * 2 + c
        part = lax.rem(e, 2)
        return remote(kv.at[slot, part], kv.at[slot, part], down_s.at[e], down_r.at[e], below)

    def down_arrival(e):
        slot = lax.rem(y + 1 + lax.div(e, 2), CHIPS) * 2 + c
        part = lax.rem(e, 2)
        return remote(kv.at[slot, part], kv.at[slot, part], down_s.at[e], down_r.at[e], below), slot, part

    def up_sends(e):
        return (y < CHIPS - 1) & (y - lax.div(e, 2) >= 0)

    def up_gets(e):
        return y - 1 - lax.div(e, 2) >= 0

    def down_sends(e):
        return lax.rem(y + lax.div(e, 2), CHIPS) < CHIPS - DOWN_STEPS

    def down_gets(e):
        return lax.rem(y + 1 + lax.div(e, 2), CHIPS) < CHIPS - DOWN_STEPS

    def down_keeps(e):
        return (y + 1 + lax.div(e, 2) >= CHIPS) & down_gets(e)

    def kv_sib(i, slot, part):
        return remote(kv.at[slot, part], kv.at[slot, part], kvsib_s.at[i], kvsib_r.at[i], other)

    UP0, DOWN0 = 2, 2 + 2 * UP_STEPS

    for load in loads[:3]:
        load.wait()
    raw = dtr[...]
    dt = jnp.maximum(raw, 0.0) + jnp.log1p(jnp.exp(-jnp.abs(raw)))
    rate = jnp.exp(alog[...])
    row = lax.broadcasted_iota(jnp.int32, (BLK, BLK), 0)
    col = lax.broadcasted_iota(jnp.int32, (BLK, BLK), 1)
    tri = row >= col
    cum = lax.dot_general(
        tri.astype(F32), -dt * rate, (((1,), (0,)), ((), ())), precision=lax.Precision.HIGHEST,
        preferred_element_type=F32,
    )
    w_hi, w_lo = split(dt * jnp.exp(-cum))
    u_hi, u_lo = split(jnp.exp(cum))
    s_hi, s_lo = split(jnp.broadcast_to(skip[...], (16, SSM_HEADS)))
    for i, part in enumerate((w_hi, w_lo, u_hi, u_lo)):
        stack[pl.ds(i * BLK, BLK), :] = part
    stack[pl.ds(4 * BLK, 16), :] = s_hi
    stack[pl.ds(4 * BLK + 16, 16), :] = s_lo
    for load in loads[3:5]:
        load.wait()

    def expansion(j):
        heads = HALF // HEAD_P
        r = lax.broadcasted_iota(jnp.int32, (SSM_HEADS, HALF), 0)
        k = lax.broadcasted_iota(jnp.int32, (SSM_HEADS, HALF), 1)
        return (r - j * heads == lax.shift_right_logical(k, 6)).astype(F32).astype(BF16)

    def own_state(j, carry):
        g, half = lax.div(j, 2), lax.rem(j, 2)
        cols = pl.ds(pl.multiple_of(j * HALF, HALF), HALF)
        wide = dot(stack[pl.ds(0, 4 * BLK), :], expansion(j))
        w = wide[0:BLK] + wide[BLK : 2 * BLK]
        uu = wide[2 * BLK : 3 * BLK] + wide[3 * BLK : 4 * BLK]
        scaled = (x[:, cols].astype(F32) * w).astype(BF16)
        xs[:, cols] = scaled
        u[:, cols] = uu
        last = uu[BLK - 1 : BLK, :]
        bt = jnp.transpose(b[:, pl.ds(pl.multiple_of(g * BLK, BLK), BLK)].astype(F32)).astype(BF16)
        state = dot(bt, scaled) * last
        for i in range(4):
            piece = slice(i * PIECE, (i + 1) * PIECE)
            local[half, g * 4 + i] = state[:, piece].astype(BF16)
            dec[half, g * 4 + i] = jnp.broadcast_to(last[:, piece], (8, PIECE))
        return carry

    lax.fori_loop(0, 2 * GROUPS, own_state, 0)

    for load in loads[5:7]:
        load.wait()
    pl.semaphore_wait(barrier, 3)

    ex_d = remote(dec, dsib, ex_s.at[0], ex_r.at[0], other)
    ex_chain = remote(local.at[oc], sib.at[oc], ex_s.at[1], ex_r.at[1], other)
    ex_chain_in = remote(local.at[c], sib.at[c], ex_s.at[1], ex_r.at[1], other)
    ex_rest = remote(local.at[0], sib.at[0], ex_s.at[2], ex_r.at[2], other)
    ex_d.start()
    ex_chain.start()

    for e in range(2):
        @pl.when(down_sends(e))
        def _(e=e):
            down_copy(e).start()

        @pl.when(up_sends(e))
        def _(e=e):
            up_copy(e).start()

    @pl.when(c == 0)
    def _():
        ex_rest.start()

    for e in range(2):
        kv_sib(e, me, e).start()

    ex_d.wait()
    ex_chain.wait_send()
    ex_chain_in.wait_recv()
    first = (c == 0).astype(F32)

    def chip_state(k, carry):
        mine, theirs = local[c, k].astype(F32), sib[c, k].astype(F32)
        d_mine, d_theirs = dec[c, k][0:1, :], dsib[c, k][0:1, :]
        value = first * (d_theirs * mine + theirs) + (1.0 - first) * (d_mine * theirs + mine)
        chip[k] = value

        @pl.when(y == 0)
        def _():
            isend[k] = value.astype(BF16)
            pin[c, k] = jnp.zeros((BLK, PIECE), BF16)
            remote(isend.at[k], pin.at[c, k], chain_s.at[k], chain_r.at[k], above).start()
            remote(pin.at[c, k], pin.at[c, k], psib_s.at[k], psib_r.at[k], other).start()

        return carry

    lax.fori_loop(0, CHUNKS, chip_state, 0)

    for load in loads[7:]:
        load.wait()

    def own_part(j, carry):
        g = lax.div(j, 2)
        cols = pl.ds(pl.multiple_of(j * HALF, HALF), HALF)
        state_cols = pl.ds(pl.multiple_of(g * BLK, BLK), BLK)
        wide = dot(stack[pl.ds(4 * BLK, 32), :], expansion(j))
        sk = wide[0:1] + wide[16:17]
        products = dot_t(cp[:, state_cols], b[:, state_cols])
        mixing = jnp.where(tri, products, 0.0).astype(BF16)
        uu = u[:, cols]
        base = uu * dot(mixing, xs[:, cols]) + sk * x[:, cols].astype(F32)
        gt = gate[:, cols].astype(F32)
        act = gt / (1.0 + jnp.exp(-gt))
        a1[:, cols] = base * act
        a2[:, cols] = uu * act
        return carry

    lax.fori_loop(0, 2 * GROUPS, own_part, 0)

    def attention(kh):
        blocks = [lists[0, i] for i in range(3)]
        slots = [jnp.where(i < 0, me, i) for i in blocks]
        biases = [jnp.where(i < 0, MASKED, 0.0).astype(F32) for i in blocks]
        cols = pl.ds(pl.multiple_of(kh * HEAD_D, HEAD_D), HEAD_D)
        queries = jnp.concatenate(
            [q[:, pl.ds(pl.multiple_of((kh * RATIO + i) * HEAD_D, HEAD_D), HEAD_D)] for i in range(RATIO)], axis=0
        )
        scale = HEAD_D ** (-0.5)
        tri4 = jnp.concatenate([tri] * RATIO, axis=0)
        scores = [jnp.where(tri4, dot_t(queries, kv[me, 0, :, cols]) * scale, MASKED)]
        for slot, bias in zip(slots, biases):
            scores.append(dot_t(queries, kv[slot, 0, :, cols]) * scale + bias)
        top = scores[0]
        for s in scores[1:]:
            top = jnp.maximum(top, s)
        top = jnp.max(top, axis=1, keepdims=True)
        weights = [jnp.exp(s - top) for s in scores]
        total = weights[0] + weights[1] + weights[2] + weights[3]
        total = jnp.sum(total, axis=1, keepdims=True)
        acc = dot(weights[0].astype(BF16), kv[me, 1, :, cols])
        for slot, weight in zip(slots, weights[1:]):
            acc = acc + dot(weight.astype(BF16), kv[slot, 1, :, cols])
        out = (acc / total).astype(BF16)
        for i in range(RATIO):
            attn_v[:, pl.ds(pl.multiple_of((kh * RATIO + i) * HEAD_D, HEAD_D), HEAD_D)] = out[i * BLK : (i + 1) * BLK]

    reach = lax.div(y * LAG_NUM, LAG_DEN)
    attn_at = jnp.where(y == CHIPS - 1, ATTN_LAST, jnp.maximum(reach + CHUNKS + 1, ATTN_FIRST))

    def tick(t, carry):
        k = t - reach

        @pl.when((y > 0) & (k >= 0) & (k < CHUNKS))
        def _():
            into = remote(isend.at[k], pin.at[c, k], chain_s.at[k], chain_r.at[k], above)
            into.wait_recv()

            @pl.when(y < CHIPS - 1)
            def _():
                d = dec[c, k][0:1, :] * dsib[c, k][0:1, :]
                isend[k] = (d * pin[c, k].astype(F32) + chip[k]).astype(BF16)
                into.start()

            remote(pin.at[c, k], pin.at[c, k], psib_s.at[k], psib_r.at[k], other).start()

        e = lax.div(t, KV_TICKS) - 1
        now = (lax.rem(t, KV_TICKS) == 0) & (e >= 0)

        @pl.when(now & (e < 2 * DOWN_STEPS) & down_gets(jnp.maximum(e, 0)))
        def _():
            arrival, slot, part = down_arrival(e)
            arrival.wait_recv()

            @pl.when(e < 2 * DOWN_STEPS - 2)
            def _():
                down_copy(e + 2).start()

            @pl.when(down_keeps(e))
            def _():
                kv_sib(DOWN0 + e, slot, part).start()

        @pl.when(now & (e < 2 * UP_STEPS) & up_gets(jnp.maximum(e, 0)))
        def _():
            arrival, slot, part = up_arrival(e)
            arrival.wait_recv()

            @pl.when((e < 2 * UP_STEPS - 2) & (y < CHIPS - 1))
            def _():
                up_copy(e + 2).start()

            kv_sib(UP0 + e, slot, part).start()

        @pl.when(t == attn_at)
        def _():
            def wait_sib(i, carry):
                kv_sib(i, me, 0).wait_recv()
                return carry

            lax.fori_loop(0, 2, wait_sib, 0)

            def wait_up(i, carry):
                @pl.when(up_gets(i))
                def _():
                    kv_sib(UP0 + i, me, 0).wait_recv()
                return carry

            def wait_down(i, carry):
                @pl.when(down_keeps(i))
                def _():
                    kv_sib(DOWN0 + i, me, 0).wait_recv()
                return carry

            lax.fori_loop(0, 2 * UP_STEPS, wait_up, 0)
            lax.fori_loop(0, 2 * DOWN_STEPS, wait_down, 0)

        @pl.when((t >= attn_at) & (t < attn_at + KVHEADS))
        def _():
            attention(t - attn_at)

        return carry

    lax.fori_loop(0, TICKS, tick, 0)
    attn_out = pltpu.make_async_copy(attn_v, attn_hbm, out_sem.at[0])
    attn_out.start()

    @pl.when(c == 1)
    def _():
        ex_rest.wait_recv()

    def finish(g, carry):
        cols = pl.ds(pl.multiple_of(g * COLS, COLS), COLS)
        state_cols = pl.ds(pl.multiple_of(g * BLK, BLK), BLK)
        for i in range(4):
            k = g * 4 + i
            remote(pin.at[oc, k], pin.at[oc, k], psib_s.at[k], psib_r.at[k], other).wait_recv()
        for half in range(2):
            for i in range(4):
                k = g * 4 + i

                @pl.when(c == 0)
                def _(half=half, i=i, k=k):
                    enter[:, (half * 4 + i) * PIECE : (half * 4 + i + 1) * PIECE] = pin[half, k]

                @pl.when(c == 1)
                def _(half=half, i=i, k=k):
                    came = dsib[half, k][0:1, :] * pin[half, k].astype(F32) + sib[half, k].astype(F32)
                    enter[:, (half * 4 + i) * PIECE : (half * 4 + i + 1) * PIECE] = came.astype(BF16)

        gated = a1[:, cols] + a2[:, cols] * dot(cp[:, state_cols], enter[...])
        square = jnp.sum(gated * gated, axis=1, keepdims=True)
        scale = lax.rsqrt(square * (1.0 / COLS) + NORM_EPS)
        ssm_v[:, cols] = (gated * scale * gain[:, cols]).astype(BF16)
        return carry

    lax.fori_loop(0, GROUPS, finish, 0)
    ssm_out = pltpu.make_async_copy(ssm_v, ssm_hbm, out_sem.at[1])
    ssm_out.start()

    @pl.when(c == 0)
    def _():
        ex_rest.wait_send()

    def wait_chain(k, carry):
        remote(pin.at[c, k], pin.at[c, k], psib_s.at[k], psib_r.at[k], other).wait_send()

        @pl.when(y < CHIPS - 1)
        def _():
            remote(isend.at[k], pin.at[c, k], chain_s.at[k], chain_r.at[k], above).wait_send()
        return carry

    lax.fori_loop(0, CHUNKS, wait_chain, 0)

    def wait_up_sent(e, carry):
        @pl.when(up_sends(e))
        def _():
            up_copy(e).wait_send()

        @pl.when(up_gets(e))
        def _():
            kv_sib(UP0 + e, me, 0).wait_send()
        return carry

    def wait_down_sent(e, carry):
        @pl.when(down_sends(e))
        def _():
            down_copy(e).wait_send()

        @pl.when(down_keeps(e))
        def _():
            kv_sib(DOWN0 + e, me, 0).wait_send()
        return carry

    lax.fori_loop(0, 2 * UP_STEPS, wait_up_sent, 0)
    lax.fori_loop(0, 2 * DOWN_STEPS, wait_down_sent, 0)
    for e in range(2):
        kv_sib(e, me, e).wait_send()
    attn_out.wait()
    ssm_out.wait()


def body(ssm_input, gate_input, b_proj, c_proj, dt_raw, a_log, skip, norm_gain, queries, keys, values, block_lists):
    vmem = pltpu.VMEM
    dma = lambda n: pltpu.SemaphoreType.DMA((n,))
    wide = GROUPS * COLS
    any_spec = pl.BlockSpec(memory_space=pl.ANY)
    return pl.pallas_call(
        kernel,
        out_shape=(
            jax.ShapeDtypeStruct((BLK, wide), BF16),
            jax.ShapeDtypeStruct((BLK, KVHEADS * RATIO * HEAD_D), BF16),
        ),
        in_specs=[any_spec] * 12,
        out_specs=(any_spec, any_spec),
        scratch_shapes=[
            vmem((BLK, wide), BF16), vmem((BLK, wide), BF16), vmem((BLK, GROUPS * BLK), BF16),
            vmem((BLK, GROUPS * BLK), BF16), vmem((BLK, SSM_HEADS), F32), vmem((1, SSM_HEADS), F32),
            vmem((1, SSM_HEADS), F32), vmem((1, wide), F32), vmem((BLK, KVHEADS * RATIO * HEAD_D), BF16),
            pltpu.SMEM((1, 3), jnp.int32),
            vmem((2 * CHIPS, 2, BLK, KVHEADS * HEAD_D), BF16),
            vmem((4 * BLK + 32, SSM_HEADS), BF16),
            vmem((BLK, wide), BF16), vmem((BLK, wide), F32), vmem((BLK, wide), F32), vmem((BLK, wide), F32),
            vmem((2, CHUNKS, BLK, PIECE), BF16), vmem((2, CHUNKS, BLK, PIECE), BF16),
            vmem((2, CHUNKS, 8, PIECE), F32), vmem((2, CHUNKS, 8, PIECE), F32),
            vmem((CHUNKS, BLK, PIECE), F32), vmem((CHUNKS, BLK, PIECE), BF16),
            vmem((2, CHUNKS, BLK, PIECE), BF16), vmem((BLK, COLS), BF16),
            vmem((BLK, wide), BF16), vmem((BLK, KVHEADS * RATIO * HEAD_D), BF16),
            dma(12), dma(2),
            dma(2 * UP_STEPS), dma(2 * UP_STEPS), dma(2 * DOWN_STEPS), dma(2 * DOWN_STEPS),
            dma(2 + 2 * UP_STEPS + 2 * DOWN_STEPS), dma(2 + 2 * UP_STEPS + 2 * DOWN_STEPS),
            dma(CHUNKS), dma(CHUNKS), dma(CHUNKS), dma(CHUNKS), dma(3), dma(3),
        ],
        compiler_params=pltpu.CompilerParams(
            collective_id=0, has_side_effects=True, vmem_limit_bytes=48 * 2**20
        ),
        name="layers",
    )(
        ssm_input, gate_input, b_proj, c_proj, dt_raw, a_log.reshape(1, -1), skip.reshape(1, -1),
        norm_gain.reshape(1, -1), queries, keys, values, block_lists,
    )


def solution(mesh):
    rows = P(("dp", "ctx"), None)
    in_specs = (rows, rows, rows, rows, rows, P(), P(), P(), rows, rows, rows, rows)
    return jax.shard_map(body, mesh=mesh, in_specs=in_specs, out_specs=(rows, rows), check_vma=False)
```

time: 309 us -> 67.3 us (0.22)
  the two profiles are of different devices: /device:TPU:69 before, /device:TPU:48 now
where the time goes in v1:
time: 67.3 us; the launch traced here: 66.9 us
  Pallas kernels  56.4 us (84%)
  local copies, waits for them, and re-layouts  9.75 us (14%)
  between operations  0.72 us (1%)
    pallas_call x1, Pallas kernels, body(): pl.pallas_call(kernel, out_shape=(jax.ShapeDtypeStruct((BLK, wide), BF16)...  56.4 us
    unnamed x25, local copies, waits for them, and re-layouts  9.75 us

profile of v1, /device:TPU:48, one launch (start us, length us, event | category | flops | bytes accessed | tf_op | source)
XLA Modules:
  0.0 66.9 jit_solution(1872301006868912176)
XLA Ops:
  0.6 0.0 copy-start.7
  0.6 0.0 copy-start.8
  0.7 0.0 copy-start.9
  0.7 0.0 copy-start.10
  0.7 0.9 %copy.14.dt_hbm = f32[128,64]{1,0:T(8,128)S(1)} copy(f32[128,64]{0,1:T(8,128)} %param.16) | data formatting | bytes 65536 | tf_op args[4]
  1.5 0.0 copy-done.7
  1.6 0.0 copy-done.8
  1.6 0.0 copy-done.9
  1.6 0.0 copy-done.10
  1.6 0.0 copy-start
  1.6 1.2 %copy-done = bf16[128,4096]{1,0:T(8,128)(2,1)S(1)} copy-done((bf16[128,4096]{1,0:T(8,128)(2,1)S(1)}, bf16[128,4096]{1,0:T(8,128)(2,1)}, u32[]{:S(2)}) %copy-start) | copy-done | bytes 1048600
  2.8 0.0 copy-start.1
  2.8 1.2 %copy-done.1 = bf16[128,4096]{1,0:T(8,128)(2,1)S(1)} copy-done((bf16[128,4096]{1,0:T(8,128)(2,1)S(1)}, bf16[128,4096]{1,0:T(8,128)(2,1)}, u32[]{:S(2)}) %copy-start.1) | copy-done | bytes 1048600
  4.0 0.0 copy-start.2
  4.0 1.0 %copy-done.2 = bf16[128,2048]{1,0:T(8,128)(2,1)S(1)} copy-done((bf16[128,2048]{1,0:T(8,128)(2,1)S(1)}, bf16[128,2048]{1,0:T(8,128)(2,1)}, u32[]{:S(2)}) %copy-start.2) | copy-done | bytes 524312
  5.1 0.0 copy-start.3
  5.1 0.9 %copy-done.3 = bf16[128,512]{1,0:T(8,128)(2,1)S(1)} copy-done((bf16[128,512]{1,0:T(8,128)(2,1)S(1)}, bf16[128,512]{1,0:T(8,128)(2,1)}, u32[]{:S(2)}) %copy-start.3) | copy-done | bytes 131096
  6.0 0.0 copy-start.4
  6.0 0.9 %copy-done.4 = bf16[128,512]{1,0:T(8,128)(2,1)S(1)} copy-done((bf16[128,512]{1,0:T(8,128)(2,1)S(1)}, bf16[128,512]{1,0:T(8,128)(2,1)}, u32[]{:S(2)}) %copy-start.4) | copy-done | bytes 131096
  6.9 0.0 copy-start.5
  6.9 0.9 %copy-done.5 = bf16[128,512]{1,0:T(8,128)(2,1)S(1)} copy-done((bf16[128,512]{1,0:T(8,128)(2,1)S(1)}, bf16[128,512]{1,0:T(8,128)(2,1)}, u32[]{:S(2)}) %copy-start.5) | copy-done | bytes 131096
  7.8 0.0 copy-start.6
  7.8 0.9 %copy-done.6 = bf16[128,512]{1,0:T(8,128)(2,1)S(1)} copy-done((bf16[128,512]{1,0:T(8,128)(2,1)S(1)}, bf16[128,512]{1,0:T(8,128)(2,1)}, u32[]{:S(2)}) %copy-start.6) | copy-done | bytes 131096
  8.7 56.4 %layers.1 = (bf16[128,4096]{1,0:T(8,128)(2,1)S(1)}, bf16[128,2048]{1,0:T(8,128)(2,1)S(1)}) custom-call(bf16[128,4096]{1,0:T(8,128)(2,1)S(1)} %copy-done, bf16[128,4096]{1,0:T(8,128)(2,1)S(1)} %copy-done.1, bf16[128,512]{1,0:T(8,128)(2,1)S(1)} %copy-done.3, bf16[128,512]{1,0:T(8,128)(2,1)S(1)} %copy-done.4, f32[128,64]{1,0:T(8,128)S(1)} %copy.14.dt_hbm, ...), custom_call_target="tpu_custom_call" | custom-call | tf_op jit(solution)/shard_map/layers/pallas_call | solution.py:431
  65.1 1.0 %copy.17 = bf16[128,4096]{1,0:T(8,128)(2,1)} copy(bf16[128,4096]{1,0:T(8,128)(2,1)S(1)} %get-tuple-element.4) | data formatting | bytes 2097152
  66.1 0.8 %copy.18 = bf16[128,2048]{1,0:T(8,128)(2,1)} copy(bf16[128,2048]{1,0:T(8,128)(2,1)S(1)} %get-tuple-element.5) | data formatting | bytes 1048576
Async XLA Ops:
  0.6 0.9 %copy-start.7 = (f32[4096]{0:T(1024)S(1)}, f32[4096]{0:T(1024)}, u32[]{:S(2)}) copy-start(f32[4096]{0:T(1024)} %param.19) | copy-start | bytes 49156
  0.6 0.9 %copy-start.8 = (f32[64]{0:T(128)S(1)}, f32[64]{0:T(128)}, u32[]{:S(2)}) copy-start(f32[64]{0:T(128)} %param.17) | copy-start | bytes 772
  0.7 0.9 %copy-start.9 = (f32[64]{0:T(128)S(1)}, f32[64]{0:T(128)}, u32[]{:S(2)}) copy-start(f32[64]{0:T(128)} %param.18) | copy-start | bytes 772
  0.7 0.9 %copy-start.10 = (s32[1,3]{1,0:T(1,128)S(1)}, s32[1,3]{1,0:T(1,128)}, u32[]{:S(2)}) copy-start(s32[1,3]{1,0:T(1,128)} %list_hbm.1) | copy-start | bytes 40
  1.6 1.2 %copy-start = (bf16[128,4096]{1,0:T(8,128)(2,1)S(1)}, bf16[128,4096]{1,0:T(8,128)(2,1)}, u32[]{:S(2)}) copy-start(bf16[128,4096]{1,0:T(8,128)(2,1)} %x_hbm.1) | copy-start | bytes 3145732
  2.8 1.2 %copy-start.1 = (bf16[128,4096]{1,0:T(8,128)(2,1)S(1)}, bf16[128,4096]{1,0:T(8,128)(2,1)}, u32[]{:S(2)}) copy-start(bf16[128,4096]{1,0:T(8,128)(2,1)} %gate_hbm.1) | copy-start | bytes 3145732
  4.0 1.0 %copy-start.2 = (bf16[128,2048]{1,0:T(8,128)(2,1)S(1)}, bf16[128,2048]{1,0:T(8,128)(2,1)}, u32[]{:S(2)}) copy-start(bf16[128,2048]{1,0:T(8,128)(2,1)} %q_hbm.1) | copy-start | bytes 1572868
  5.1 0.9 %copy-start.3 = (bf16[128,512]{1,0:T(8,128)(2,1)S(1)}, bf16[128,512]{1,0:T(8,128)(2,1)}, u32[]{:S(2)}) copy-start(bf16[128,512]{1,0:T(8,128)(2,1)} %b_hbm.1) | copy-start | bytes 393220
  6.0 0.9 %copy-start.4 = (bf16[128,512]{1,0:T(8,128)(2,1)S(1)}, bf16[128,512]{1,0:T(8,128)(2,1)}, u32[]{:S(2)}) copy-start(bf16[128,512]{1,0:T(8,128)(2,1)} %c_hbm.1) | copy-start | bytes 393220
  6.9 0.9 %copy-start.5 = (bf16[128,512]{1,0:T(8,128)(2,1)S(1)}, bf16[128,512]{1,0:T(8,128)(2,1)}, u32[]{:S(2)}) copy-start(bf16[128,512]{1,0:T(8,128)(2,1)} %k_hbm.1) | copy-start | bytes 393220
  7.8 0.9 %copy-start.6 = (bf16[128,512]{1,0:T(8,128)(2,1)S(1)}, bf16[128,512]{1,0:T(8,128)(2,1)}, u32[]{:S(2)}) copy-start(bf16[128,512]{1,0:T(8,128)(2,1)} %v_hbm.1) | copy-start | bytes 393220

commit v2 on v1

v2 whole, which is shorter than its diff:
```python
import jax
import jax.numpy as jnp
from jax import lax
from jax.experimental import pallas as pl
from jax.experimental.pallas import tpu as pltpu
from jax.sharding import PartitionSpec as P

MESH = pl.DeviceIdType.MESH
F32 = jnp.float32
BF16 = jnp.bfloat16

SSM_HEADS = 64
HEAD_P = 64
GROUPS = 4
KVHEADS = 4
RATIO = 4
HEAD_D = 128
BLK = 128
NORM_EPS = 1e-05
MASKED = -1e30

CHIPS = 8
HALF = 512
COLS = 1024
PIECE = 128
PER_GROUP = 4
CHUNKS = GROUPS * PER_GROUP
UP_STEPS = 3
DOWN_STEPS = 5
LAG_NUM, LAG_DEN = 9, 2
KV_TICKS = 4
ATTN_TICK = (26, 22, 31, 41, 41, 41, 33, 33)
ATTN_HEADS = 2
STORES = 2
ATTN_PIECES = KVHEADS * RATIO // ATTN_HEADS


def dot(a, b):
    return lax.dot_general(a, b, (((1,), (0,)), ((), ())), preferred_element_type=F32)


def dot_t(a, b):
    return lax.dot_general(a, b, (((1,), (1,)), ((), ())), preferred_element_type=F32)


def split(v):
    hi = v.astype(BF16)
    return hi, (v - hi.astype(F32)).astype(BF16)


def pick(y, table):
    value = table[0]
    for i in range(1, CHIPS):
        value = jnp.where(y == i, table[i], value)
    return value


def kernel(
    x_hbm, gate_hbm, b_hbm, c_hbm, dt_hbm, alog_hbm, skip_hbm, gain_hbm, q_hbm, k_hbm, v_hbm, list_hbm,
    ssm_hbm, attn_hbm,
    x, gate, b, cp, dtr, alog, skip, gain, q, lists,
    kv, stack, spread, bt, xs, a1, a2, local, sib, dec, dsib, chip, isend, pin, enter, ssm_v, attn_v,
    in_sem, out_sem,
    up_s, up_r, down_s, down_r, kvsib_s, kvsib_r, chain_s, chain_r, psib_s, psib_r, ex_s, ex_r,
):
    me = lax.axis_index("ctx")
    y = lax.div(me, 2)
    c = lax.rem(me, 2)
    oc = 1 - c
    above = lax.rem(y + 1, CHIPS) * 2 + c
    below = lax.rem(y + CHIPS - 1, CHIPS) * 2 + c
    other = y * 2 + oc

    barrier = pltpu.get_barrier_semaphore()
    for peer in (above, below, other):
        pl.semaphore_signal(barrier, inc=1, device_id={"ctx": peer}, device_id_type=MESH)

    loads = [
        pltpu.make_async_copy(src, dst, in_sem.at[i])
        for i, (src, dst) in enumerate(
            (
                (dt_hbm, dtr), (alog_hbm, alog), (skip_hbm, skip), (b_hbm, b),
                (k_hbm, kv.at[me, 0]), (v_hbm, kv.at[me, 1]), (x_hbm, x), (c_hbm, cp), (gate_hbm, gate),
                (gain_hbm, gain), (q_hbm, q), (list_hbm, lists),
            )
        )
    ]
    for load in loads:
        load.start()

    def remote(src, dst, send, recv, to):
        return pltpu.make_async_remote_copy(
            src_ref=src, dst_ref=dst, send_sem=send, recv_sem=recv, device_id={"ctx": to}, device_id_type=MESH
        )

    def up_copy(e, ahead=0):
        slot = lax.rem(y - ahead - lax.div(e, 2) + CHIPS, CHIPS) * 2 + c
        part = lax.rem(e, 2)
        return remote(kv.at[slot, part], kv.at[slot, part], up_s.at[e], up_r.at[e], above), slot, part

    def down_copy(e, ahead=0):
        slot = lax.rem(y + ahead + lax.div(e, 2), CHIPS) * 2 + c
        part = lax.rem(e, 2)
        return remote(kv.at[slot, part], kv.at[slot, part], down_s.at[e], down_r.at[e], below), slot, part

    def up_sends(e):
        step = lax.div(e, 2)
        return (y < CHIPS - 1) & (y >= step) & ((step < 2) | (y - step >= 3))

    def up_gets(e):
        step = lax.div(e, 2)
        return (y >= 1 + step) & ((step < 2) | (y - 1 - step >= 3))

    def down_goes(source, step):
        return (source < 3) | ((source == 3) & (step < 4))

    def down_sends(e):
        step = lax.div(e, 2)
        return down_goes(lax.rem(y + step, CHIPS), step)

    def down_gets(e):
        step = lax.div(e, 2)
        return down_goes(lax.rem(y + 1 + step, CHIPS), step)

    def down_keeps(e):
        return (y + 1 + lax.div(e, 2) >= CHIPS) & down_gets(e)

    def kv_sib(i, slot, part):
        return remote(kv.at[slot, part], kv.at[slot, part], kvsib_s.at[i], kvsib_r.at[i], other)

    UP0, DOWN0 = 2, 2 + 2 * UP_STEPS

    r = lax.broadcasted_iota(jnp.int32, (SSM_HEADS, HALF), 0)
    h = lax.shift_right_logical(lax.broadcasted_iota(jnp.int32, (SSM_HEADS, HALF), 1), 6)
    for j in range(2 * GROUPS):
        spread[j] = (r - j * (HALF // HEAD_P) == h).astype(F32).astype(BF16)

    for load in loads[:4]:
        load.wait()
    raw = jnp.transpose(dtr[...])
    dt = jnp.maximum(raw, 0.0) + jnp.log1p(jnp.exp(-jnp.abs(raw)))
    rate = jnp.exp(alog[...])
    row = lax.broadcasted_iota(jnp.int32, (BLK, BLK), 0)
    col = lax.broadcasted_iota(jnp.int32, (BLK, BLK), 1)
    tri = row >= col
    cum = lax.dot_general(
        tri.astype(F32), -dt * rate, (((1,), (0,)), ((), ())), precision=lax.Precision.HIGHEST,
        preferred_element_type=F32,
    )
    up_to = jnp.exp(cum)
    l_hi, l_lo = split(jnp.broadcast_to(up_to[BLK - 1 : BLK], (16, SSM_HEADS)))
    s_hi, s_lo = split(jnp.broadcast_to(skip[...], (16, SSM_HEADS)))
    stack[0:BLK, :] = (dt * jnp.exp(-cum)).astype(BF16)
    stack[BLK : BLK + 16, :] = l_hi
    stack[BLK + 16 : BLK + 32, :] = l_lo
    stack[BLK + 32 : 2 * BLK + 32, :] = up_to.astype(BF16)
    stack[2 * BLK + 32 : 2 * BLK + 48, :] = s_hi
    stack[2 * BLK + 48 : 2 * BLK + 64, :] = s_lo
    for g in range(GROUPS):
        bt[g] = jnp.transpose(b[:, g * BLK : (g + 1) * BLK].astype(F32)).astype(BF16)
    for load in loads[4:7]:
        load.wait()

    pl.semaphore_wait(barrier, 3)
    for e in range(2):
        @pl.when(down_sends(e))
        def _(e=e):
            down_copy(e)[0].start()

        @pl.when(up_sends(e))
        def _(e=e):
            up_copy(e)[0].start()

    def ex_d(g):
        some = pl.ds(g * PER_GROUP, PER_GROUP)
        return remote(dec.at[some], dsib.at[some], ex_s.at[g], ex_r.at[g], other)

    def ex_half(g, half):
        some = pl.ds(g * PER_GROUP, PER_GROUP)
        i = GROUPS + g
        return remote(local.at[half, some], sib.at[half, some], ex_s.at[i], ex_r.at[i], other)

    ex_rest = remote(local.at[0], sib.at[0], ex_s.at[2 * GROUPS], ex_r.at[2 * GROUPS], other)
    first = (c == 0).astype(F32)

    def own_state(g):
        for half in range(2):
            j = 2 * g + half
            cols = pl.ds(j * HALF, HALF)
            wide = dot(stack[0 : BLK + 32, :], spread[j])
            scaled = (x[:, cols].astype(F32) * wide[0:BLK]).astype(BF16)
            xs[:, cols] = scaled
            last = wide[BLK : BLK + 1] + wide[BLK + 16 : BLK + 17]
            state = dot(bt[g], scaled) * last
            for i in range(PER_GROUP):
                piece = slice(i * PIECE, (i + 1) * PIECE)
                local[half, g * PER_GROUP + i] = state[:, piece].astype(BF16)
                dec[g * PER_GROUP + i, half] = jnp.broadcast_to(last[:, piece], (8, PIECE))

    def chip_state(g):
        ex_d(g).wait_recv()
        ex_half(g, c).wait_recv()

        def one(i, carry):
            k = g * PER_GROUP + i
            mine, theirs = local[c, k].astype(F32), sib[c, k].astype(F32)
            d_mine, d_theirs = dec[k, c][0:1, :], dsib[k, c][0:1, :]
            value = first * (d_theirs * mine + theirs) + (1.0 - first) * (d_mine * theirs + mine)
            chip[k] = value

            @pl.when(y == 0)
            def _():
                isend[k] = value.astype(BF16)
                remote(isend.at[k], pin.at[c, k], chain_s.at[k], chain_r.at[k], above).start()
                pin[0, k] = jnp.zeros((BLK, PIECE), BF16)
                pin[1, k] = jnp.zeros((BLK, PIECE), BF16)

            return carry

        lax.fori_loop(0, PER_GROUP, one, 0)

    for g in range(GROUPS):
        own_state(g)
        ex_d(g).start()
        ex_half(g, oc).start()
        if g > 0:
            chip_state(g - 1)
    chip_state(GROUPS - 1)

    @pl.when(c == 0)
    def _():
        ex_rest.start()

    for e in range(2):
        kv_sib(e, me, e).start()

    for load in loads[7:]:
        load.wait()

    def own_part(j, carry):
        g = lax.div(j, 2)
        cols = pl.ds(pl.multiple_of(j * HALF, HALF), HALF)
        state_cols = pl.ds(pl.multiple_of(g * BLK, BLK), BLK)
        wide = dot(stack[BLK + 32 : 2 * BLK + 64, :], spread[j])
        uu = wide[0:BLK]
        sk = wide[BLK : BLK + 1] + wide[BLK + 16 : BLK + 17]
        products = dot_t(cp[:, state_cols], b[:, state_cols])
        mixing = jnp.where(tri, products, 0.0).astype(BF16)
        base = uu * dot(mixing, xs[:, cols]) + sk * x[:, cols].astype(F32)
        gt = gate[:, cols].astype(F32)
        act = gt / (1.0 + jnp.exp(-gt))
        a1[:, cols] = base * act
        a2[:, cols] = uu * act
        return carry

    lax.fori_loop(0, 2 * GROUPS, own_part, 0)

    def attention(piece):
        blocks = [lists[0, i] for i in range(3)]
        slots = [me] + [jnp.where(i < 0, me, i) for i in blocks]
        biases = [jnp.where(i < 0, MASKED, 0.0).astype(F32) for i in blocks]
        kh = lax.div(piece * ATTN_HEADS, RATIO)
        cols = pl.ds(pl.multiple_of(kh * HEAD_D, HEAD_D), HEAD_D)
        heads = [
            pl.ds(pl.multiple_of((piece * ATTN_HEADS + i) * HEAD_D, HEAD_D), HEAD_D) for i in range(ATTN_HEADS)
        ]
        queries = jnp.concatenate([q[:, head] for head in heads], axis=0)
        scale = HEAD_D ** (-0.5)
        tris = jnp.concatenate([tri] * ATTN_HEADS, axis=0)
        scores = [dot_t(queries, kv[slot, 0, :, cols]) * scale for slot in slots]
        scores = [jnp.where(tris, scores[0], MASKED)] + [s + bias for s, bias in zip(scores[1:], biases)]
        top = jnp.maximum(jnp.maximum(scores[0], scores[1]), jnp.maximum(scores[2], scores[3]))
        top = jnp.max(top, axis=1, keepdims=True)
        weights = [jnp.exp(s - top) for s in scores]
        total = (weights[0] + weights[1]) + (weights[2] + weights[3])
        total = jnp.sum(total, axis=1, keepdims=True)
        acc = dot(weights[0].astype(BF16), kv[slots[0], 1, :, cols])
        for slot, weight in zip(slots[1:], weights[1:]):
            acc = acc + dot(weight.astype(BF16), kv[slot, 1, :, cols])
        out = (acc / total).astype(BF16)
        for i, head in enumerate(heads):
            attn_v[:, head] = out[i * BLK : (i + 1) * BLK]

    def psib(half, k):
        return remote(pin.at[half, k], pin.at[half, k], psib_s.at[k], psib_r.at[k], other)

    def finish(g):
        @pl.when((c == 1) & (g == 0))
        def _():
            ex_rest.wait_recv()

        cols = pl.ds(pl.multiple_of(g * COLS, COLS), COLS)
        state_cols = pl.ds(pl.multiple_of(g * BLK, BLK), BLK)

        @pl.when(y > 0)
        def _():
            for i in range(PER_GROUP):
                psib(oc, g * PER_GROUP + i).wait_recv()

        for half in range(2):
            for i in range(PER_GROUP):
                k = g * PER_GROUP + i
                place = slice((half * PER_GROUP + i) * PIECE, (half * PER_GROUP + i + 1) * PIECE)

                @pl.when(c == 0)
                def _(half=half, k=k, place=place):
                    enter[:, place] = pin[half, k]

                @pl.when(c == 1)
                def _(half=half, k=k, place=place):
                    came = dsib[k, half][0:1, :] * pin[half, k].astype(F32) + sib[half, k].astype(F32)
                    enter[:, place] = came.astype(BF16)

        gated = a1[:, cols] + a2[:, cols] * dot(cp[:, state_cols], enter[...])
        square = jnp.sum(gated * gated, axis=1, keepdims=True)
        scale = lax.rsqrt(square * (1.0 / COLS) + NORM_EPS)
        ssm_v[:, cols] = (gated * scale * gain[:, cols]).astype(BF16)

    reach = lax.div(y * LAG_NUM, LAG_DEN)
    attn_at = pick(y, ATTN_TICK)
    end = jnp.maximum(reach + CHUNKS + 2, attn_at + ATTN_PIECES)
    late = (y == 1) | (y == 2)
    late_from = (y == 2) | (y == 3)

    def tick(t, carry):
        k = t - reach

        @pl.when((y > 0) & (k >= 0) & (k < CHUNKS))
        def _():
            into = remote(isend.at[k], pin.at[c, k], chain_s.at[k], chain_r.at[k], above)
            into.wait_recv()

            @pl.when(y < CHIPS - 1)
            def _():
                d = dec[k, c][0:1, :] * dsib[k, c][0:1, :]
                isend[k] = (d * pin[c, k].astype(F32) + chip[k]).astype(BF16)
                into.start()

            psib(c, k).start()

        @pl.when(late & (k == CHUNKS))
        def _():
            for e in (2, 3):
                up_copy(e)[0].start()

        @pl.when((k >= PER_GROUP + 1) & (lax.rem(k, PER_GROUP) == 1) & (k <= CHUNKS + 1))
        def _():
            finish(lax.div(k, PER_GROUP) - 1)

        e = lax.div(t, KV_TICKS) - 1
        now = (lax.rem(t, KV_TICKS) == 0) & (e >= 0)

        @pl.when(now & (e < 2 * DOWN_STEPS) & down_gets(jnp.maximum(e, 0)))
        def _():
            arrival, slot, part = down_copy(e, 1)
            arrival.wait_recv()

            @pl.when((e < 2 * DOWN_STEPS - 2) & down_sends(e + 2))
            def _():
                down_copy(e + 2)[0].start()

            @pl.when(down_keeps(e))
            def _():
                kv_sib(DOWN0 + e, slot, part).start()

        behind = late_from & (k >= CHUNKS + 1) & (k < CHUNKS + 3)
        u = jnp.where(behind, k - CHUNKS + 1, e)
        due = behind | (now & (e < 2 * UP_STEPS) & (jnp.logical_not(late_from) | (e < 2)))

        @pl.when(due & up_gets(jnp.maximum(u, 0)))
        def _():
            arrival, slot, part = up_copy(u, 1)
            arrival.wait_recv()

            @pl.when((u < 2 * UP_STEPS - 2) & up_sends(u + 2) & jnp.logical_not(late))
            def _():
                up_copy(u + 2)[0].start()

            kv_sib(UP0 + u, slot, part).start()

        @pl.when(t == attn_at)
        def _():
            for i in range(2):
                kv_sib(i, me, 0).wait_recv()

            def wait_up(i, carry):
                @pl.when(up_gets(i))
                def _():
                    kv_sib(UP0 + i, me, 0).wait_recv()
                return carry

            def wait_down(i, carry):
                @pl.when(down_keeps(i))
                def _():
                    kv_sib(DOWN0 + i, me, 0).wait_recv()
                return carry

            lax.fori_loop(0, 2 * UP_STEPS, wait_up, 0)
            lax.fori_loop(0, 2 * DOWN_STEPS, wait_down, 0)

        @pl.when((t >= attn_at) & (t < attn_at + ATTN_PIECES))
        def _():
            attention(t - attn_at)

        return carry

    lax.fori_loop(0, end, tick, 0)
    attn_out = pltpu.make_async_copy(attn_v, attn_hbm, out_sem.at[0])
    attn_out.start()
    ssm_out = pltpu.make_async_copy(ssm_v, ssm_hbm, out_sem.at[1])
    ssm_out.start()

    @pl.when(c == 0)
    def _():
        ex_rest.wait_send()

    for g in range(GROUPS):
        ex_d(g).wait_send()
        ex_half(g, oc).wait_send()

    def wait_chain(k, carry):
        @pl.when(y > 0)
        def _():
            psib(c, k).wait_send()

        @pl.when(y < CHIPS - 1)
        def _():
            remote(isend.at[k], pin.at[c, k], chain_s.at[k], chain_r.at[k], above).wait_send()
        return carry

    lax.fori_loop(0, CHUNKS, wait_chain, 0)

    def wait_up_sent(e, carry):
        @pl.when(up_sends(e))
        def _():
            up_copy(e)[0].wait_send()

        @pl.when(up_gets(e))
        def _():
            kv_sib(UP0 + e, me, 0).wait_send()
        return carry

    def wait_down_sent(e, carry):
        @pl.when(down_sends(e))
        def _():
            down_copy(e)[0].wait_send()

        @pl.when(down_keeps(e))
        def _():
            kv_sib(DOWN0 + e, me, 0).wait_send()
        return carry

    lax.fori_loop(0, 2 * UP_STEPS, wait_up_sent, 0)
    lax.fori_loop(0, 2 * DOWN_STEPS, wait_down_sent, 0)
    for e in range(2):
        kv_sib(e, me, e).wait_send()
    attn_out.wait()
    ssm_out.wait()


def store_kernel(ssm, attn, ssm_out, attn_out, ssm_v, attn_v, sem):
    parts = []
    for src, mid, dst in ((ssm, ssm_v, ssm_out), (attn, attn_v, attn_out)):
        for i in range(STORES):
            rows = pl.ds(i * (BLK // STORES), BLK // STORES)
            n = 2 * len(parts)
            parts.append(
                (
                    pltpu.make_async_copy(src.at[rows], mid.at[rows], sem.at[n]),
                    pltpu.make_async_copy(mid.at[rows], dst.at[rows], sem.at[n + 1]),
                )
            )
    for load, _ in parts:
        load.start()
    for load, store in parts:
        load.wait()
        store.start()
    for _, store in parts:
        store.wait()


def body(ssm_input, gate_input, b_proj, c_proj, dt_raw, a_log, skip, norm_gain, queries, keys, values, block_lists):
    vmem = pltpu.VMEM
    dma = lambda n: pltpu.SemaphoreType.DMA((n,))
    wide = GROUPS * COLS
    heads = KVHEADS * RATIO * HEAD_D
    any_spec = pl.BlockSpec(memory_space=pl.ANY)
    outs = (jax.ShapeDtypeStruct((BLK, wide), BF16), jax.ShapeDtypeStruct((BLK, heads), BF16))
    ssm, attn = pl.pallas_call(
        kernel,
        out_shape=outs,
        in_specs=[any_spec] * 12,
        out_specs=(any_spec, any_spec),
        scratch_shapes=[
            vmem((BLK, wide), BF16), vmem((BLK, wide), BF16), vmem((BLK, GROUPS * BLK), BF16),
            vmem((BLK, GROUPS * BLK), BF16), vmem((SSM_HEADS, BLK), F32), vmem((1, SSM_HEADS), F32),
            vmem((1, SSM_HEADS), F32), vmem((1, wide), F32), vmem((BLK, heads), BF16),
            pltpu.SMEM((1, 3), jnp.int32),
            vmem((2 * CHIPS, 2, BLK, KVHEADS * HEAD_D), BF16),
            vmem((2 * BLK + 64, SSM_HEADS), BF16), vmem((2 * GROUPS, SSM_HEADS, HALF), BF16),
            vmem((GROUPS, BLK, BLK), BF16),
            vmem((BLK, wide), BF16), vmem((BLK, wide), F32), vmem((BLK, wide), F32),
            vmem((2, CHUNKS, BLK, PIECE), BF16), vmem((2, CHUNKS, BLK, PIECE), BF16),
            vmem((CHUNKS, 2, 8, PIECE), F32), vmem((CHUNKS, 2, 8, PIECE), F32),
            vmem((CHUNKS, BLK, PIECE), F32), vmem((CHUNKS, BLK, PIECE), BF16),
            vmem((2, CHUNKS, BLK, PIECE), BF16), vmem((BLK, COLS), BF16),
            vmem((BLK, wide), BF16), vmem((BLK, heads), BF16),
            dma(12), dma(2),
            dma(2 * UP_STEPS), dma(2 * UP_STEPS), dma(2 * DOWN_STEPS), dma(2 * DOWN_STEPS),
            dma(2 + 2 * UP_STEPS + 2 * DOWN_STEPS), dma(2 + 2 * UP_STEPS + 2 * DOWN_STEPS),
            dma(CHUNKS), dma(CHUNKS), dma(CHUNKS), dma(CHUNKS), dma(2 * GROUPS + 1), dma(2 * GROUPS + 1),
        ],
        compiler_params=pltpu.CompilerParams(
            collective_id=0, has_side_effects=True, vmem_limit_bytes=63 * 2**20
        ),
        name="layers",
    )(
        ssm_input, gate_input, b_proj, c_proj, dt_raw.T, a_log.reshape(1, -1), skip.reshape(1, -1),
        norm_gain.reshape(1, -1), queries, keys, values, block_lists,
    )
    return pl.pallas_call(
        store_kernel,
        out_shape=outs,
        in_specs=[any_spec] * 2,
        out_specs=(any_spec, any_spec),
        scratch_shapes=[vmem((BLK, wide), BF16), vmem((BLK, heads), BF16), dma(4 * STORES)],
        compiler_params=pltpu.CompilerParams(vmem_limit_bytes=63 * 2**20),
        name="store",
    )(ssm, attn)


def solution(mesh):
    rows = P(("dp", "ctx"), None)
    in_specs = (rows, rows, rows, rows, rows, P(), P(), P(), rows, rows, rows, rows)
    return jax.shard_map(body, mesh=mesh, in_specs=in_specs, out_specs=(rows, rows), check_vma=False)
```

time: 67.3 us -> 53.9 us (0.80)
  the two profiles are of different devices: /device:TPU:48 before, /device:TPU:57 now
where the time goes in v2:
time: 53.9 us; the launch traced here: 53.8 us
  Pallas kernels  53.1 us (99%)
  between operations  0.64 us (1%)
    pallas_call x1, Pallas kernels, body(): pl.pallas_call(kernel, out_shape=outs, in_specs=[any_spec] * 12, out_spec...  50.9 us
    pallas_call x1, Pallas kernels, body(): pl.pallas_call(store_kernel, out_shape=outs, in_specs=[any_spec] * 2, out...  2.25 us

profile of v2, /device:TPU:57, one launch (start us, length us, event | category | flops | bytes accessed | tf_op | source)
XLA Modules:
  0.0 53.8 jit_solution(1508344700455291561)
XLA Ops:
  0.6 50.9 %layers.1 = (bf16[128,4096]{1,0:T(8,128)(2,1)}, bf16[128,2048]{1,0:T(8,128)(2,1)}) custom-call(bf16[128,4096]{1,0:T(8,128)(2,1)} %x_hbm.1, bf16[128,4096]{1,0:T(8,128)(2,1)} %gate_hbm.1, bf16[128,512]{1,0:T(8,128)(2,1)} %b_hbm.1, bf16[128,512]{1,0:T(8,128)(2,1)} %c_hbm.1, f32[64,128]{1,0:T(8,128)} %bitcast.4, f32[1,64]{1,0:T(1,128)} %bitcast.6, ...), custom_call_target="tpu_custom_call" | custom-call | tf_op jit(solution)/shard_map/layers/pallas_call | solution.py:489
  51.5 2.2 %store.1 = (bf16[128,4096]{1,0:T(8,128)(2,1)}, bf16[128,2048]{1,0:T(8,128)(2,1)}) custom-call(bf16[128,4096]{1,0:T(8,128)(2,1)} %get-tuple-element.4.ssm, bf16[128,2048]{1,0:T(8,128)(2,1)} %get-tuple-element.5.attn), custom_call_target="tpu_custom_call" | custom-call | tf_op jit(solution)/shard_map/store/pallas_call | solution.py:521

commit v3 on v2

--- a/solution.py
+++ b/solution.py
@@ -28,8 +28,10 @@
 UP_STEPS = 3
 DOWN_STEPS = 5
 LAG_NUM, LAG_DEN = 9, 2
-KV_TICKS = 4
-ATTN_TICK = (26, 22, 31, 41, 41, 41, 33, 33)
+KV_PARTS = 4
+KV_ROWS = 2 * BLK // KV_PARTS
+KV_TICKS = 2
+ATTN_TICK = (26, 26, 31, 41, 41, 41, 44, 33)
 ATTN_HEADS = 2
 STORES = 2
 ATTN_PIECES = KVHEADS * RATIO // ATTN_HEADS
@@ -57,10 +59,10 @@
 
 def kernel(
     x_hbm, gate_hbm, b_hbm, c_hbm, dt_hbm, alog_hbm, skip_hbm, gain_hbm, q_hbm, k_hbm, v_hbm, list_hbm,
-    ssm_hbm, attn_hbm,
+    ssm_v, attn_v,
     x, gate, b, cp, dtr, alog, skip, gain, q, lists,
-    kv, stack, spread, bt, xs, a1, a2, local, sib, dec, dsib, chip, isend, pin, enter, ssm_v, attn_v,
-    in_sem, out_sem,
+    kv, stack, spread, bt, xs, a1, a2, local, sib, dec, dsib, chip, isend, pin, enter,
+    in_sem,
     up_s, up_r, down_s, down_r, kvsib_s, kvsib_r, chain_s, chain_r, psib_s, psib_r, ex_s, ex_r,
 ):
     me = lax.axis_index("ctx")
@@ -93,42 +95,46 @@
             src_ref=src, dst_ref=dst, send_sem=send, recv_sem=recv, device_id={"ctx": to}, device_id_type=MESH
         )
 
+    def kv_part(slot, part):
+        rows = lax.rem(part, 2) * KV_ROWS
+        return kv.at[slot, lax.div(part, 2), pl.ds(pl.multiple_of(rows, KV_ROWS), KV_ROWS)]
+
     def up_copy(e, ahead=0):
-        slot = lax.rem(y - ahead - lax.div(e, 2) + CHIPS, CHIPS) * 2 + c
-        part = lax.rem(e, 2)
-        return remote(kv.at[slot, part], kv.at[slot, part], up_s.at[e], up_r.at[e], above), slot, part
+        slot = lax.rem(y - ahead - lax.div(e, KV_PARTS) + CHIPS, CHIPS) * 2 + c
+        part = lax.rem(e, KV_PARTS)
+        return remote(kv_part(slot, part), kv_part(slot, part), up_s.at[e], up_r.at[e], above), slot, part
 
     def down_copy(e, ahead=0):
-        slot = lax.rem(y + ahead + lax.div(e, 2), CHIPS) * 2 + c
-        part = lax.rem(e, 2)
-        return remote(kv.at[slot, part], kv.at[slot, part], down_s.at[e], down_r.at[e], below), slot, part
+        slot = lax.rem(y + ahead + lax.div(e, KV_PARTS), CHIPS) * 2 + c
+        part = lax.rem(e, KV_PARTS)
+        return remote(kv_part(slot, part), kv_part(slot, part), down_s.at[e], down_r.at[e], below), slot, part
 
     def up_sends(e):
-        step = lax.div(e, 2)
+        step = lax.div(e, KV_PARTS)
         return (y < CHIPS - 1) & (y >= step) & ((step < 2) | (y - step >= 3))
 
     def up_gets(e):
-        step = lax.div(e, 2)
+        step = lax.div(e, KV_PARTS)
         return (y >= 1 + step) & ((step < 2) | (y - 1 - step >= 3))
 
     def down_goes(source, step):
         return (source < 3) | ((source == 3) & (step < 4))
 
     def down_sends(e):
-        step = lax.div(e, 2)
+        step = lax.div(e, KV_PARTS)
         return down_goes(lax.rem(y + step, CHIPS), step)
 
     def down_gets(e):
-        step = lax.div(e, 2)
+        step = lax.div(e, KV_PARTS)
         return down_goes(lax.rem(y + 1 + step, CHIPS), step)
 
     def down_keeps(e):
-        return (y + 1 + lax.div(e, 2) >= CHIPS) & down_gets(e)
+        return (y + 1 + lax.div(e, KV_PARTS) >= CHIPS) & down_gets(e)
 
     def kv_sib(i, slot, part):
-        return remote(kv.at[slot, part], kv.at[slot, part], kvsib_s.at[i], kvsib_r.at[i], other)
-
-    UP0, DOWN0 = 2, 2 + 2 * UP_STEPS
+        return remote(kv_part(slot, part), kv_part(slot, part), kvsib_s.at[i], kvsib_r.at[i], other)
+
+    UP0, DOWN0 = KV_PARTS, KV_PARTS + KV_PARTS * UP_STEPS
 
     r = lax.broadcasted_iota(jnp.int32, (SSM_HEADS, HALF), 0)
     h = lax.shift_right_logical(lax.broadcasted_iota(jnp.int32, (SSM_HEADS, HALF), 1), 6)
@@ -162,12 +168,12 @@
         load.wait()
 
     pl.semaphore_wait(barrier, 3)
-    for e in range(2):
+    for e in range(KV_PARTS):
         @pl.when(down_sends(e))
         def _(e=e):
             down_copy(e)[0].start()
 
-        @pl.when(up_sends(e))
+        @pl.when(up_sends(e) & (y > 0))
         def _(e=e):
             up_copy(e)[0].start()
 
@@ -211,7 +217,7 @@
             @pl.when(y == 0)
             def _():
                 isend[k] = value.astype(BF16)
-                remote(isend.at[k], pin.at[c, k], chain_s.at[k], chain_r.at[k], above).start()
+                remote(isend.at[k], pin.at[c, k], chain_s.at[0], chain_r.at[k], above).start()
                 pin[0, k] = jnp.zeros((BLK, PIECE), BF16)
                 pin[1, k] = jnp.zeros((BLK, PIECE), BF16)
 
@@ -227,17 +233,22 @@
             chip_state(g - 1)
     chip_state(GROUPS - 1)
 
+    @pl.when(y == 0)
+    def _():
+        for e in range(KV_PARTS):
+            up_copy(e)[0].start()
+
     @pl.when(c == 0)
     def _():
         ex_rest.start()
 
-    for e in range(2):
+    for e in range(KV_PARTS):
         kv_sib(e, me, e).start()
 
     for load in loads[7:]:
         load.wait()
 
-    def own_part(j, carry):
+    def own_part(j):
         g = lax.div(j, 2)
         cols = pl.ds(pl.multiple_of(j * HALF, HALF), HALF)
         state_cols = pl.ds(pl.multiple_of(g * BLK, BLK), BLK)
@@ -251,9 +262,6 @@
         act = gt / (1.0 + jnp.exp(-gt))
         a1[:, cols] = base * act
         a2[:, cols] = uu * act
-        return carry
-
-    lax.fori_loop(0, 2 * GROUPS, own_part, 0)
 
     def attention(piece):
         blocks = [lists[0, i] for i in range(3)]
@@ -282,7 +290,7 @@
             attn_v[:, head] = out[i * BLK : (i + 1) * BLK]
 
     def psib(half, k):
-        return remote(pin.at[half, k], pin.at[half, k], psib_s.at[k], psib_r.at[k], other)
+        return remote(pin.at[half, k], pin.at[half, k], psib_s.at[0], psib_r.at[k], other)
 
     def finish(g):
         @pl.when((c == 1) & (g == 0))
@@ -318,16 +326,18 @@
 
     reach = lax.div(y * LAG_NUM, LAG_DEN)
     attn_at = pick(y, ATTN_TICK)
-    end = jnp.maximum(reach + CHUNKS + 2, attn_at + ATTN_PIECES)
-    late = (y == 1) | (y == 2)
-    late_from = (y == 2) | (y == 3)
+    end = jnp.maximum(reach + CHUNKS + 1 + GROUPS, attn_at + ATTN_PIECES + 1)
+    last_chip = y == CHIPS - 1
+    late = y == 2
+    late_from = (y >= 1) & (y <= 3)
+    late_event = jnp.where(y == 1, 0, KV_PARTS)
 
     def tick(t, carry):
         k = t - reach
 
         @pl.when((y > 0) & (k >= 0) & (k < CHUNKS))
         def _():
-            into = remote(isend.at[k], pin.at[c, k], chain_s.at[k], chain_r.at[k], above)
+            into = remote(isend.at[k], pin.at[c, k], chain_s.at[0], chain_r.at[k], above)
             into.wait_recv()
 
             @pl.when(y < CHIPS - 1)
@@ -338,49 +348,56 @@
 
             psib(c, k).start()
 
+        @pl.when(t < 2 * GROUPS)
+        def _():
+            own_part(t)
+
         @pl.when(late & (k == CHUNKS))
         def _():
-            for e in (2, 3):
+            for e in range(KV_PARTS, 2 * KV_PARTS):
                 up_copy(e)[0].start()
 
-        @pl.when((k >= PER_GROUP + 1) & (lax.rem(k, PER_GROUP) == 1) & (k <= CHUNKS + 1))
-        def _():
-            finish(lax.div(k, PER_GROUP) - 1)
+        in_chain = last_chip & (k > PER_GROUP) & (lax.rem(k, PER_GROUP) == 1) & (k <= CHUNKS + 1)
+        behind_chain = jnp.logical_not(last_chip) & (k > CHUNKS) & (k <= CHUNKS + GROUPS)
+
+        @pl.when(in_chain | behind_chain)
+        def _():
+            finish(jnp.where(last_chip, lax.div(k, PER_GROUP) - 1, k - CHUNKS - 1))
 
         e = lax.div(t, KV_TICKS) - 1
         now = (lax.rem(t, KV_TICKS) == 0) & (e >= 0)
 
-        @pl.when(now & (e < 2 * DOWN_STEPS) & down_gets(jnp.maximum(e, 0)))
+        @pl.when(now & (e < KV_PARTS * DOWN_STEPS) & down_gets(jnp.maximum(e, 0)))
         def _():
             arrival, slot, part = down_copy(e, 1)
             arrival.wait_recv()
 
-            @pl.when((e < 2 * DOWN_STEPS - 2) & down_sends(e + 2))
+            @pl.when((e < KV_PARTS * (DOWN_STEPS - 1)) & down_sends(e + KV_PARTS))
             def _():
-                down_copy(e + 2)[0].start()
+                down_copy(e + KV_PARTS)[0].start()
 
             @pl.when(down_keeps(e))
             def _():
                 kv_sib(DOWN0 + e, slot, part).start()
 
-        behind = late_from & (k >= CHUNKS + 1) & (k < CHUNKS + 3)
-        u = jnp.where(behind, k - CHUNKS + 1, e)
-        due = behind | (now & (e < 2 * UP_STEPS) & (jnp.logical_not(late_from) | (e < 2)))
+        behind = late_from & (k > CHUNKS) & (k <= CHUNKS + KV_PARTS)
+        u = jnp.where(behind, k - CHUNKS - 1 + late_event, e)
+        due = behind | (now & (e < KV_PARTS * UP_STEPS) & (jnp.logical_not(late_from) | (e < late_event)))
 
         @pl.when(due & up_gets(jnp.maximum(u, 0)))
         def _():
             arrival, slot, part = up_copy(u, 1)
             arrival.wait_recv()
 
-            @pl.when((u < 2 * UP_STEPS - 2) & up_sends(u + 2) & jnp.logical_not(late))
+            @pl.when((u < KV_PARTS * (UP_STEPS - 1)) & up_sends(u + KV_PARTS) & jnp.logical_not(late))
             def _():
-                up_copy(u + 2)[0].start()
+                up_copy(u + KV_PARTS)[0].start()
 
             kv_sib(UP0 + u, slot, part).start()
 
         @pl.when(t == attn_at)
         def _():
-            for i in range(2):
+            for i in range(KV_PARTS):
                 kv_sib(i, me, 0).wait_recv()
 
             def wait_up(i, carry):
@@ -395,88 +412,71 @@
                     kv_sib(DOWN0 + i, me, 0).wait_recv()
                 return carry
 
-            lax.fori_loop(0, 2 * UP_STEPS, wait_up, 0)
-            lax.fori_loop(0, 2 * DOWN_STEPS, wait_down, 0)
+            lax.fori_loop(0, KV_PARTS * UP_STEPS, wait_up, 0)
+            lax.fori_loop(0, KV_PARTS * DOWN_STEPS, wait_down, 0)
 
         @pl.when((t >= attn_at) & (t < attn_at + ATTN_PIECES))
         def _():
             attention(t - attn_at)
 
+        @pl.when(t == attn_at + ATTN_PIECES)
+        def _():
+            @pl.when(c == 0)
+            def _():
+                ex_rest.wait_send()
+
+            for g in range(GROUPS):
+                ex_d(g).wait_send()
+                ex_half(g, oc).wait_send()
+
+            def wait_up_sent(i, carry):
+                @pl.when(up_sends(i))
+                def _():
+                    up_copy(i)[0].wait_send()
+
+                @pl.when(up_gets(i))
+                def _():
+                    kv_sib(UP0 + i, me, 0).wait_send()
+                return carry
+
+            def wait_down_sent(i, carry):
+                @pl.when(down_sends(i))
+                def _():
+                    down_copy(i)[0].wait_send()
+
+                @pl.when(down_keeps(i))
+                def _():
+                    kv_sib(DOWN0 + i, me, 0).wait_send()
+                return carry
+
+            lax.fori_loop(0, KV_PARTS * UP_STEPS, wait_up_sent, 0)
+            lax.fori_loop(0, KV_PARTS * DOWN_STEPS, wait_down_sent, 0)
+            for i in range(KV_PARTS):
+                kv_sib(i, me, i).wait_send()
+
         return carry
 
     lax.fori_loop(0, end, tick, 0)
-    attn_out = pltpu.make_async_copy(attn_v, attn_hbm, out_sem.at[0])
-    attn_out.start()
-    ssm_out = pltpu.make_async_copy(ssm_v, ssm_hbm, out_sem.at[1])
-    ssm_out.start()
-
-    @pl.when(c == 0)
+
+    @pl.when(y > 0)
     def _():
-        ex_rest.wait_send()
-
-    for g in range(GROUPS):
-        ex_d(g).wait_send()
-        ex_half(g, oc).wait_send()
-
-    def wait_chain(k, carry):
-        @pl.when(y > 0)
-        def _():
-            psib(c, k).wait_send()
-
-        @pl.when(y < CHIPS - 1)
-        def _():
-            remote(isend.at[k], pin.at[c, k], chain_s.at[k], chain_r.at[k], above).wait_send()
-        return carry
-
-    lax.fori_loop(0, CHUNKS, wait_chain, 0)
-
-    def wait_up_sent(e, carry):
-        @pl.when(up_sends(e))
-        def _():
-            up_copy(e)[0].wait_send()
-
-        @pl.when(up_gets(e))
-        def _():
-            kv_sib(UP0 + e, me, 0).wait_send()
-        return carry
-
-    def wait_down_sent(e, carry):
-        @pl.when(down_sends(e))
-        def _():
-            down_copy(e)[0].wait_send()
-
-        @pl.when(down_keeps(e))
-        def _():
-            kv_sib(DOWN0 + e, me, 0).wait_send()
-        return carry
-
-    lax.fori_loop(0, 2 * UP_STEPS, wait_up_sent, 0)
-    lax.fori_loop(0, 2 * DOWN_STEPS, wait_down_sent, 0)
-    for e in range(2):
-        kv_sib(e, me, e).wait_send()
-    attn_out.wait()
-    ssm_out.wait()
-
-
-def store_kernel(ssm, attn, ssm_out, attn_out, ssm_v, attn_v, sem):
-    parts = []
-    for src, mid, dst in ((ssm, ssm_v, ssm_out), (attn, attn_v, attn_out)):
+        remote(pin.at[c], pin.at[c], psib_s.at[0], psib_r.at[0], other).wait_send()
+
+    @pl.when(y < CHIPS - 1)
+    def _():
+        remote(isend, pin.at[c], chain_s.at[0], chain_r.at[0], above).wait_send()
+
+
+def store_kernel(ssm, attn, ssm_out, attn_out, sem):
+    copies = []
+    for src, dst in ((ssm, ssm_out), (attn, attn_out)):
         for i in range(STORES):
             rows = pl.ds(i * (BLK // STORES), BLK // STORES)
-            n = 2 * len(parts)
-            parts.append(
-                (
-                    pltpu.make_async_copy(src.at[rows], mid.at[rows], sem.at[n]),
-                    pltpu.make_async_copy(mid.at[rows], dst.at[rows], sem.at[n + 1]),
-                )
-            )
-    for load, _ in parts:
-        load.start()
-    for load, store in parts:
-        load.wait()
-        store.start()
-    for _, store in parts:
-        store.wait()
+            copies.append(pltpu.make_async_copy(src.at[rows], dst.at[rows], sem.at[len(copies)]))
+    for copy in copies:
+        copy.start()
+    for copy in copies:
+        copy.wait()
 
 
 def body(ssm_input, gate_input, b_proj, c_proj, dt_raw, a_log, skip, norm_gain, queries, keys, values, block_lists):
@@ -485,12 +485,13 @@
     wide = GROUPS * COLS
     heads = KVHEADS * RATIO * HEAD_D
     any_spec = pl.BlockSpec(memory_space=pl.ANY)
+    vmem_spec = pl.BlockSpec(memory_space=pltpu.VMEM)
     outs = (jax.ShapeDtypeStruct((BLK, wide), BF16), jax.ShapeDtypeStruct((BLK, heads), BF16))
     ssm, attn = pl.pallas_call(
         kernel,
-        out_shape=outs,
+        out_shape=(vmem((BLK, wide), BF16), vmem((BLK, heads), BF16)),
         in_specs=[any_spec] * 12,
-        out_specs=(any_spec, any_spec),
+        out_specs=(vmem_spec, vmem_spec),
         scratch_shapes=[
             vmem((BLK, wide), BF16), vmem((BLK, wide), BF16), vmem((BLK, GROUPS * BLK), BF16),
             vmem((BLK, GROUPS * BLK), BF16), vmem((SSM_HEADS, BLK), F32), vmem((1, SSM_HEADS), F32),
@@ -504,14 +505,14 @@
             vmem((CHUNKS, 2, 8, PIECE), F32), vmem((CHUNKS, 2, 8, PIECE), F32),
             vmem((CHUNKS, BLK, PIECE), F32), vmem((CHUNKS, BLK, PIECE), BF16),
             vmem((2, CHUNKS, BLK, PIECE), BF16), vmem((BLK, COLS), BF16),
-            vmem((BLK, wide), BF16), vmem((BLK, heads), BF16),
-            dma(12), dma(2),
-            dma(2 * UP_STEPS), dma(2 * UP_STEPS), dma(2 * DOWN_STEPS), dma(2 * DOWN_STEPS),
-            dma(2 + 2 * UP_STEPS + 2 * DOWN_STEPS), dma(2 + 2 * UP_STEPS + 2 * DOWN_STEPS),
-            dma(CHUNKS), dma(CHUNKS), dma(CHUNKS), dma(CHUNKS), dma(2 * GROUPS + 1), dma(2 * GROUPS + 1),
+            dma(12),
+            dma(KV_PARTS * UP_STEPS), dma(KV_PARTS * UP_STEPS), dma(KV_PARTS * DOWN_STEPS),
+            dma(KV_PARTS * DOWN_STEPS), dma(KV_PARTS * (1 + UP_STEPS + DOWN_STEPS)),
+            dma(KV_PARTS * (1 + UP_STEPS + DOWN_STEPS)),
+            dma(1), dma(CHUNKS), dma(1), dma(CHUNKS), dma(2 * GROUPS + 1), dma(2 * GROUPS + 1),
         ],
         compiler_params=pltpu.CompilerParams(
-            collective_id=0, has_side_effects=True, vmem_limit_bytes=63 * 2**20
+            collective_id=0, has_side_effects=True, vmem_limit_bytes=60 * 2**20
         ),
         name="layers",
     )(
@@ -521,10 +522,10 @@
     return pl.pallas_call(
         store_kernel,
         out_shape=outs,
-        in_specs=[any_spec] * 2,
+        in_specs=[vmem_spec] * 2,
         out_specs=(any_spec, any_spec),
-        scratch_shapes=[vmem((BLK, wide), BF16), vmem((BLK, heads), BF16), dma(4 * STORES)],
-        compiler_params=pltpu.CompilerParams(vmem_limit_bytes=63 * 2**20),
+        scratch_shapes=[dma(2 * STORES)],
+        compiler_params=pltpu.CompilerParams(vmem_limit_bytes=4 * 2**20),
         name="store",
     )(ssm, attn)
 

time: 53.9 us -> 50.4 us (0.935)
  the two profiles are of different devices: /device:TPU:57 before, /device:TPU:48 now
where the time goes in v3:
time: 50.4 us; the launch traced here: 50.3 us
  Pallas kernels  49.6 us (98%)
  between operations  0.64 us (1%)
    pallas_call x1, Pallas kernels, body(): pl.pallas_call(kernel, out_shape=(vmem((BLK, wide), BF16), vmem((BLK, hea...  48.4 us
    pallas_call x1, Pallas kernels, body(): pl.pallas_call(store_kernel, out_shape=outs, in_specs=[vmem_spec] * 2, ou...  1.17 us

profile of v3, /device:TPU:48, one launch (start us, length us, event | category | flops | bytes accessed | tf_op | source)
XLA Modules:
  0.0 50.3 jit_solution(8733399770372224678)
XLA Ops:
  0.6 48.4 %layers.1 = (bf16[128,4096]{1,0:T(8,128)(2,1)S(1)}, bf16[128,2048]{1,0:T(8,128)(2,1)S(1)}) custom-call(bf16[128,4096]{1,0:T(8,128)(2,1)} %x_hbm.1, bf16[128,4096]{1,0:T(8,128)(2,1)} %gate_hbm.1, bf16[128,512]{1,0:T(8,128)(2,1)} %b_hbm.1, bf16[128,512]{1,0:T(8,128)(2,1)} %c_hbm.1, f32[64,128]{1,0:T(8,128)} %bitcast.4, f32[1,64]{1,0:T(1,128)} %bitcast.6, ...), custom_call_target="tpu_custom_call" | custom-call | tf_op jit(solution)/shard_map/layers/pallas_call | solution.py:490
  49.1 1.2 %store.1 = (bf16[128,4096]{1,0:T(8,128)(2,1)}, bf16[128,2048]{1,0:T(8,128)(2,1)}) custom-call(bf16[128,4096]{1,0:T(8,128)(2,1)S(1)} %get-tuple-element.4.ssm, bf16[128,2048]{1,0:T(8,128)(2,1)S(1)} %get-tuple-element.5.attn), custom_call_target="tpu_custom_call" | custom-call | tf_op jit(solution)/shard_map/store/pallas_call | solution.py:522

commit v4 on v3

--- a/solution.py
+++ b/solution.py
@@ -18,6 +18,7 @@
 BLK = 128
 NORM_EPS = 1e-05
 MASKED = -1e30
+LOG2_E = 1.4426950408889634
 
 CHIPS = 8
 HALF = 512
@@ -25,6 +26,8 @@
 PIECE = 128
 PER_GROUP = 4
 CHUNKS = GROUPS * PER_GROUP
+CUTS = 2
+CUT = BLK // CUTS
 UP_STEPS = 3
 DOWN_STEPS = 5
 LAG_NUM, LAG_DEN = 9, 2
@@ -32,9 +35,10 @@
 KV_ROWS = 2 * BLK // KV_PARTS
 KV_TICKS = 2
 ATTN_TICK = (26, 26, 31, 41, 41, 41, 44, 33)
-ATTN_HEADS = 2
+DRAIN_TICK = (28, 28, 33, 43, 43, 43, 42, 41)
+ATTN_KEY_HEADS = 2
 STORES = 2
-ATTN_PIECES = KVHEADS * RATIO // ATTN_HEADS
+ATTN_PIECES = KVHEADS // ATTN_KEY_HEADS
 
 
 def dot(a, b):
@@ -61,7 +65,7 @@
     x_hbm, gate_hbm, b_hbm, c_hbm, dt_hbm, alog_hbm, skip_hbm, gain_hbm, q_hbm, k_hbm, v_hbm, list_hbm,
     ssm_v, attn_v,
     x, gate, b, cp, dtr, alog, skip, gain, q, lists,
-    kv, stack, spread, bt, xs, a1, a2, local, sib, dec, dsib, chip, isend, pin, enter,
+    kv, stack, spread, bt, xs, a1, a2, local, sib, dec, dsib, chip, isend, pin,
     in_sem,
     up_s, up_r, down_s, down_r, kvsib_s, kvsib_r, chain_s, chain_r, psib_s, psib_r, ex_s, ex_r,
 ):
@@ -111,22 +115,19 @@
 
     def up_sends(e):
         step = lax.div(e, KV_PARTS)
-        return (y < CHIPS - 1) & (y >= step) & ((step < 2) | (y - step >= 3))
+        return (y < CHIPS - 1) & (y >= step) & ((step < 2) | (y - step >= 4))
 
     def up_gets(e):
         step = lax.div(e, KV_PARTS)
-        return (y >= 1 + step) & ((step < 2) | (y - 1 - step >= 3))
-
-    def down_goes(source, step):
-        return (source < 3) | ((source == 3) & (step < 4))
+        return (y >= 1 + step) & ((step < 2) | (y - 1 - step >= 4))
 
     def down_sends(e):
         step = lax.div(e, KV_PARTS)
-        return down_goes(lax.rem(y + step, CHIPS), step)
+        return lax.rem(y + step, CHIPS) < CHIPS // 2
 
     def down_gets(e):
         step = lax.div(e, KV_PARTS)
-        return down_goes(lax.rem(y + 1 + step, CHIPS), step)
+        return lax.rem(y + 1 + step, CHIPS) < CHIPS // 2
 
     def down_keeps(e):
         return (y + 1 + lax.div(e, KV_PARTS) >= CHIPS) & down_gets(e)
@@ -167,16 +168,6 @@
     for load in loads[4:7]:
         load.wait()
 
-    pl.semaphore_wait(barrier, 3)
-    for e in range(KV_PARTS):
-        @pl.when(down_sends(e))
-        def _(e=e):
-            down_copy(e)[0].start()
-
-        @pl.when(up_sends(e) & (y > 0))
-        def _(e=e):
-            up_copy(e)[0].start()
-
     def ex_d(g):
         some = pl.ds(g * PER_GROUP, PER_GROUP)
         return remote(dec.at[some], dsib.at[some], ex_s.at[g], ex_r.at[g], other)
@@ -188,6 +179,11 @@
 
     ex_rest = remote(local.at[0], sib.at[0], ex_s.at[2 * GROUPS], ex_r.at[2 * GROUPS], other)
     first = (c == 0).astype(F32)
+
+    def link(k, i):
+        rows = pl.ds(i * CUT, CUT)
+        n = k * CUTS + i
+        return remote(isend.at[k, rows], pin.at[c, k, rows], chain_s.at[0], chain_r.at[n], above)
 
     def own_state(g):
         for half in range(2):
@@ -217,7 +213,8 @@
             @pl.when(y == 0)
             def _():
                 isend[k] = value.astype(BF16)
-                remote(isend.at[k], pin.at[c, k], chain_s.at[0], chain_r.at[k], above).start()
+                for cut in range(CUTS):
+                    link(k, cut).start()
                 pin[0, k] = jnp.zeros((BLK, PIECE), BF16)
                 pin[1, k] = jnp.zeros((BLK, PIECE), BF16)
 
@@ -225,12 +222,24 @@
 
         lax.fori_loop(0, PER_GROUP, one, 0)
 
-    for g in range(GROUPS):
+    own_state(0)
+    pl.semaphore_wait(barrier, 3)
+    ex_d(0).start()
+    ex_half(0, oc).start()
+    for e in range(KV_PARTS):
+        @pl.when(down_sends(e))
+        def _(e=e):
+            down_copy(e)[0].start()
+
+        @pl.when(up_sends(e) & (y > 0))
+        def _(e=e):
+            up_copy(e)[0].start()
+
+    for g in range(1, GROUPS):
         own_state(g)
         ex_d(g).start()
         ex_half(g, oc).start()
-        if g > 0:
-            chip_state(g - 1)
+        chip_state(g - 1)
     chip_state(GROUPS - 1)
 
     @pl.when(y == 0)
@@ -267,36 +276,31 @@
         blocks = [lists[0, i] for i in range(3)]
         slots = [me] + [jnp.where(i < 0, me, i) for i in blocks]
         biases = [jnp.where(i < 0, MASKED, 0.0).astype(F32) for i in blocks]
-        kh = lax.div(piece * ATTN_HEADS, RATIO)
-        cols = pl.ds(pl.multiple_of(kh * HEAD_D, HEAD_D), HEAD_D)
-        heads = [
-            pl.ds(pl.multiple_of((piece * ATTN_HEADS + i) * HEAD_D, HEAD_D), HEAD_D) for i in range(ATTN_HEADS)
-        ]
-        queries = jnp.concatenate([q[:, head] for head in heads], axis=0)
-        scale = HEAD_D ** (-0.5)
-        tris = jnp.concatenate([tri] * ATTN_HEADS, axis=0)
-        scores = [dot_t(queries, kv[slot, 0, :, cols]) * scale for slot in slots]
-        scores = [jnp.where(tris, scores[0], MASKED)] + [s + bias for s, bias in zip(scores[1:], biases)]
-        top = jnp.maximum(jnp.maximum(scores[0], scores[1]), jnp.maximum(scores[2], scores[3]))
-        top = jnp.max(top, axis=1, keepdims=True)
-        weights = [jnp.exp(s - top) for s in scores]
-        total = (weights[0] + weights[1]) + (weights[2] + weights[3])
-        total = jnp.sum(total, axis=1, keepdims=True)
-        acc = dot(weights[0].astype(BF16), kv[slots[0], 1, :, cols])
-        for slot, weight in zip(slots[1:], weights[1:]):
-            acc = acc + dot(weight.astype(BF16), kv[slot, 1, :, cols])
-        out = (acc / total).astype(BF16)
-        for i, head in enumerate(heads):
-            attn_v[:, head] = out[i * BLK : (i + 1) * BLK]
+        tris = jnp.concatenate([tri] * RATIO, axis=0)
+        scale = HEAD_D ** (-0.5) * LOG2_E
+        for h in range(ATTN_KEY_HEADS):
+            kh = piece * ATTN_KEY_HEADS + h
+            cols = pl.ds(pl.multiple_of(kh * HEAD_D, HEAD_D), HEAD_D)
+            heads = [pl.ds(pl.multiple_of((kh * RATIO + i) * HEAD_D, HEAD_D), HEAD_D) for i in range(RATIO)]
+            queries = jnp.concatenate([q[:, head] for head in heads], axis=0)
+            keys = jnp.concatenate([kv[slot, 0, :, cols] for slot in slots], axis=0)
+            values = jnp.concatenate([kv[slot, 1, :, cols] for slot in slots], axis=0)
+            values = jnp.concatenate([values, jnp.ones(values.shape, BF16)], axis=1)
+            scores = dot_t(queries, keys)
+            scores = [scores[:, i * BLK : (i + 1) * BLK] for i in range(4)]
+            scores = [jnp.where(tris, scores[0], MASKED)] + [s + bias for s, bias in zip(scores[1:], biases)]
+            top = jnp.maximum(jnp.maximum(scores[0], scores[1]), jnp.maximum(scores[2], scores[3]))
+            top = jnp.max(top, axis=1, keepdims=True)
+            weights = jnp.concatenate([jnp.exp2((s - top) * scale).astype(BF16) for s in scores], axis=1)
+            acc = dot(weights, values)
+            out = (acc[:, :HEAD_D] / acc[:, HEAD_D:]).astype(BF16)
+            for i, head in enumerate(heads):
+                attn_v[:, head] = out[i * BLK : (i + 1) * BLK]
 
     def psib(half, k):
         return remote(pin.at[half, k], pin.at[half, k], psib_s.at[0], psib_r.at[k], other)
 
     def finish(g):
-        @pl.when((c == 1) & (g == 0))
-        def _():
-            ex_rest.wait_recv()
-
         cols = pl.ds(pl.multiple_of(g * COLS, COLS), COLS)
         state_cols = pl.ds(pl.multiple_of(g * BLK, BLK), BLK)
 
@@ -305,29 +309,34 @@
             for i in range(PER_GROUP):
                 psib(oc, g * PER_GROUP + i).wait_recv()
 
-        for half in range(2):
-            for i in range(PER_GROUP):
-                k = g * PER_GROUP + i
-                place = slice((half * PER_GROUP + i) * PIECE, (half * PER_GROUP + i + 1) * PIECE)
-
-                @pl.when(c == 0)
-                def _(half=half, k=k, place=place):
-                    enter[:, place] = pin[half, k]
-
-                @pl.when(c == 1)
-                def _(half=half, k=k, place=place):
-                    came = dsib[k, half][0:1, :] * pin[half, k].astype(F32) + sib[half, k].astype(F32)
-                    enter[:, place] = came.astype(BF16)
-
-        gated = a1[:, cols] + a2[:, cols] * dot(cp[:, state_cols], enter[...])
-        square = jnp.sum(gated * gated, axis=1, keepdims=True)
-        scale = lax.rsqrt(square * (1.0 / COLS) + NORM_EPS)
-        ssm_v[:, cols] = (gated * scale * gain[:, cols]).astype(BF16)
+        def part(state):
+            gated = a1[:, cols] + a2[:, cols] * dot(cp[:, state_cols], state)
+            square = jnp.sum(gated * gated, axis=1, keepdims=True)
+            scale = lax.rsqrt(square * (1.0 / COLS) + NORM_EPS)
+            ssm_v[:, cols] = (gated * scale * gain[:, cols]).astype(BF16)
+
+        def entering(half, i):
+            k = g * PER_GROUP + i
+            came = pin[half, k].astype(F32)
+            return (dsib[k, half][0:1, :] * came + sib[half, k].astype(F32)).astype(BF16)
+
+        pieces = [(half, i) for half in range(2) for i in range(PER_GROUP)]
+
+        @pl.when(c == 0)
+        def _():
+            part(jnp.concatenate([pin[half, g * PER_GROUP + i] for half, i in pieces], axis=1))
+
+        @pl.when(c == 1)
+        def _():
+            part(jnp.concatenate([entering(half, i) for half, i in pieces], axis=1))
+
 
     reach = lax.div(y * LAG_NUM, LAG_DEN)
     attn_at = pick(y, ATTN_TICK)
-    end = jnp.maximum(reach + CHUNKS + 1 + GROUPS, attn_at + ATTN_PIECES + 1)
     last_chip = y == CHIPS - 1
+    drain_at = pick(y, DRAIN_TICK)
+    behind = jnp.where(last_chip, CHUNKS + 2, CHUNKS + 1 + GROUPS)
+    end = jnp.maximum(jnp.maximum(reach + behind, attn_at + ATTN_PIECES), drain_at + 1)
     late = y == 2
     late_from = (y >= 1) & (y <= 3)
     late_event = jnp.where(y == 1, 0, KV_PARTS)
@@ -337,14 +346,15 @@
 
         @pl.when((y > 0) & (k >= 0) & (k < CHUNKS))
         def _():
-            into = remote(isend.at[k], pin.at[c, k], chain_s.at[0], chain_r.at[k], above)
-            into.wait_recv()
-
-            @pl.when(y < CHIPS - 1)
-            def _():
-                d = dec[k, c][0:1, :] * dsib[k, c][0:1, :]
-                isend[k] = (d * pin[c, k].astype(F32) + chip[k]).astype(BF16)
-                into.start()
+            for cut in range(CUTS):
+                link(k, cut).wait_recv()
+
+                @pl.when(y < CHIPS - 1)
+                def _(cut=cut):
+                    rows = slice(cut * CUT, (cut + 1) * CUT)
+                    d = dec[k, c][0:1, :] * dsib[k, c][0:1, :]
+                    isend[k, rows] = (d * pin[c, k, rows].astype(F32) + chip[k, rows]).astype(BF16)
+                    link(k, cut).start()
 
             psib(c, k).start()
 
@@ -358,11 +368,19 @@
                 up_copy(e)[0].start()
 
         in_chain = last_chip & (k > PER_GROUP) & (lax.rem(k, PER_GROUP) == 1) & (k <= CHUNKS + 1)
-        behind_chain = jnp.logical_not(last_chip) & (k > CHUNKS) & (k <= CHUNKS + GROUPS)
-
-        @pl.when(in_chain | behind_chain)
-        def _():
-            finish(jnp.where(last_chip, lax.div(k, PER_GROUP) - 1, k - CHUNKS - 1))
+
+        @pl.when((c == 1) & (k == jnp.where(last_chip, PER_GROUP + 1, CHUNKS + 1)))
+        def _():
+            ex_rest.wait_recv()
+
+        @pl.when(in_chain)
+        def _():
+            finish(lax.div(k, PER_GROUP) - 1)
+
+        @pl.when(jnp.logical_not(last_chip) & (k == CHUNKS + 1))
+        def _():
+            for g in range(GROUPS):
+                finish(g)
 
         e = lax.div(t, KV_TICKS) - 1
         now = (lax.rem(t, KV_TICKS) == 0) & (e >= 0)
@@ -419,7 +437,7 @@
         def _():
             attention(t - attn_at)
 
-        @pl.when(t == attn_at + ATTN_PIECES)
+        @pl.when(t == drain_at)
         def _():
             @pl.when(c == 0)
             def _():
@@ -504,12 +522,12 @@
             vmem((2, CHUNKS, BLK, PIECE), BF16), vmem((2, CHUNKS, BLK, PIECE), BF16),
             vmem((CHUNKS, 2, 8, PIECE), F32), vmem((CHUNKS, 2, 8, PIECE), F32),
             vmem((CHUNKS, BLK, PIECE), F32), vmem((CHUNKS, BLK, PIECE), BF16),
-            vmem((2, CHUNKS, BLK, PIECE), BF16), vmem((BLK, COLS), BF16),
+            vmem((2, CHUNKS, BLK, PIECE), BF16),
             dma(12),
             dma(KV_PARTS * UP_STEPS), dma(KV_PARTS * UP_STEPS), dma(KV_PARTS * DOWN_STEPS),
             dma(KV_PARTS * DOWN_STEPS), dma(KV_PARTS * (1 + UP_STEPS + DOWN_STEPS)),
             dma(KV_PARTS * (1 + UP_STEPS + DOWN_STEPS)),
-            dma(1), dma(CHUNKS), dma(1), dma(CHUNKS), dma(2 * GROUPS + 1), dma(2 * GROUPS + 1),
+            dma(1), dma(CHUNKS * CUTS), dma(1), dma(CHUNKS), dma(2 * GROUPS + 1), dma(2 * GROUPS + 1),
         ],
         compiler_params=pltpu.CompilerParams(
             collective_id=0, has_side_effects=True, vmem_limit_bytes=60 * 2**20

time: 50.4 us -> 45.6 us (0.905)
  Pallas kernels: 49.6 us -> 44.8 us
    pallas_call x1, Pallas kernels: 48.4 us -> 43.6 us  [body(): pl.pallas_call(kernel, out_shape=(vmem((BLK, wide), BF16), vmem((BLK, hea...]
where the time goes in v4:
time: 45.6 us; the launch traced here: 45.4 us
  Pallas kernels  44.8 us (98%)
  between operations  0.64 us (1%)
    pallas_call x1, Pallas kernels, body(): pl.pallas_call(kernel, out_shape=(vmem((BLK, wide), BF16), vmem((BLK, hea...  43.6 us
    pallas_call x1, Pallas kernels, body(): pl.pallas_call(store_kernel, out_shape=outs, in_specs=[vmem_spec] * 2, ou...  1.17 us

profile of v4, /device:TPU:48, one launch (start us, length us, event | category | flops | bytes accessed | tf_op | source)
XLA Modules:
  0.0 45.4 jit_solution(11484097949463932765)
XLA Ops:
  0.6 43.6 %layers.1 = (bf16[128,4096]{1,0:T(8,128)(2,1)S(1)}, bf16[128,2048]{1,0:T(8,128)(2,1)S(1)}) custom-call(bf16[128,4096]{1,0:T(8,128)(2,1)} %x_hbm.1, bf16[128,4096]{1,0:T(8,128)(2,1)} %gate_hbm.1, bf16[128,512]{1,0:T(8,128)(2,1)} %b_hbm.1, bf16[128,512]{1,0:T(8,128)(2,1)} %c_hbm.1, f32[64,128]{1,0:T(8,128)} %bitcast.4, f32[1,64]{1,0:T(1,128)} %bitcast.6, ...), custom_call_target="tpu_custom_call" | custom-call | tf_op jit(solution)/shard_map/layers/pallas_call | solution.py:508
  44.3 1.2 %store.1 = (bf16[128,4096]{1,0:T(8,128)(2,1)}, bf16[128,2048]{1,0:T(8,128)(2,1)}) custom-call(bf16[128,4096]{1,0:T(8,128)(2,1)S(1)} %get-tuple-element.4.ssm, bf16[128,2048]{1,0:T(8,128)(2,1)S(1)} %get-tuple-element.5.attn), custom_call_target="tpu_custom_call" | custom-call | tf_op jit(solution)/shard_map/store/pallas_call | solution.py:540

commit v5 on v4

--- a/solution.py
+++ b/solution.py
@@ -26,17 +26,17 @@
 PIECE = 128
 PER_GROUP = 4
 CHUNKS = GROUPS * PER_GROUP
-CUTS = 2
-CUT = BLK // CUTS
 UP_STEPS = 3
 DOWN_STEPS = 5
-LAG_NUM, LAG_DEN = 9, 2
+LAG_NUM, LAG_DEN = 10, 3
 KV_PARTS = 4
-KV_ROWS = 2 * BLK // KV_PARTS
 KV_TICKS = 2
-ATTN_TICK = (26, 26, 31, 41, 41, 41, 44, 33)
-DRAIN_TICK = (28, 28, 33, 43, 43, 43, 42, 41)
-ATTN_KEY_HEADS = 2
+KV_FIRST = 4
+LATE = 4
+FIRST_TICK = 22
+NORM_TICK = (23, 23, 22, 26, 33, 38, 37, 35)
+ATTN_TICK = (32, 28, 31, 43, 43, 43, 43, 39)
+ATTN_KEY_HEADS = 4
 STORES = 2
 ATTN_PIECES = KVHEADS // ATTN_KEY_HEADS
 
@@ -99,43 +99,53 @@
             src_ref=src, dst_ref=dst, send_sem=send, recv_sem=recv, device_id={"ctx": to}, device_id_type=MESH
         )
 
-    def kv_part(slot, part):
-        rows = lax.rem(part, 2) * KV_ROWS
-        return kv.at[slot, lax.div(part, 2), pl.ds(pl.multiple_of(rows, KV_ROWS), KV_ROWS)]
+    def kv_piece(chip_y, part):
+        return kv.at[chip_y * 2 + lax.rem(part, 2), lax.div(part, 2)]
 
     def up_copy(e, ahead=0):
-        slot = lax.rem(y - ahead - lax.div(e, KV_PARTS) + CHIPS, CHIPS) * 2 + c
-        part = lax.rem(e, KV_PARTS)
-        return remote(kv_part(slot, part), kv_part(slot, part), up_s.at[e], up_r.at[e], above), slot, part
+        from_y = lax.rem(y - ahead - lax.div(e, KV_PARTS) + CHIPS, CHIPS)
+        piece = kv_piece(from_y, lax.rem(e, KV_PARTS))
+        return remote(piece, piece, up_s.at[e], up_r.at[e], above), piece
 
     def down_copy(e, ahead=0):
-        slot = lax.rem(y + ahead + lax.div(e, KV_PARTS), CHIPS) * 2 + c
-        part = lax.rem(e, KV_PARTS)
-        return remote(kv_part(slot, part), kv_part(slot, part), down_s.at[e], down_r.at[e], below), slot, part
+        from_y = lax.rem(y + ahead + lax.div(e, KV_PARTS), CHIPS)
+        piece = kv_piece(from_y, lax.rem(e, KV_PARTS))
+        return remote(piece, piece, down_s.at[e], down_r.at[e], below), piece
+
+    def up_goes(source, e):
+        values = lax.rem(e, KV_PARTS) >= KV_PARTS // 2
+        return (e < 2 * KV_PARTS) | ((source >= 4) & values)
+
+    def down_goes(source, e):
+        keys = lax.rem(e, KV_PARTS) < KV_PARTS // 2
+        return (source < 4) | ((source == 4) & keys)
 
     def up_sends(e):
         step = lax.div(e, KV_PARTS)
-        return (y < CHIPS - 1) & (y >= step) & ((step < 2) | (y - step >= 4))
+        return (y < CHIPS - 1) & (y >= step) & up_goes(y - step, e)
 
     def up_gets(e):
         step = lax.div(e, KV_PARTS)
-        return (y >= 1 + step) & ((step < 2) | (y - 1 - step >= 4))
+        return (y >= 1 + step) & up_goes(y - 1 - step, e)
 
     def down_sends(e):
         step = lax.div(e, KV_PARTS)
-        return lax.rem(y + step, CHIPS) < CHIPS // 2
+        return down_goes(lax.rem(y + step, CHIPS), e)
 
     def down_gets(e):
         step = lax.div(e, KV_PARTS)
-        return lax.rem(y + 1 + step, CHIPS) < CHIPS // 2
+        return down_goes(lax.rem(y + 1 + step, CHIPS), e)
 
     def down_keeps(e):
         return (y + 1 + lax.div(e, KV_PARTS) >= CHIPS) & down_gets(e)
 
-    def kv_sib(i, slot, part):
-        return remote(kv_part(slot, part), kv_part(slot, part), kvsib_s.at[i], kvsib_r.at[i], other)
-
-    UP0, DOWN0 = KV_PARTS, KV_PARTS + KV_PARTS * UP_STEPS
+    def kv_sib(i, piece):
+        return remote(piece, piece, kvsib_s.at[i], kvsib_r.at[i], other)
+
+    def own_sib(i):
+        return kv_sib(i, kv.at[me, i])
+
+    UP0, DOWN0 = 2, 2 + KV_PARTS * UP_STEPS
 
     r = lax.broadcasted_iota(jnp.int32, (SSM_HEADS, HALF), 0)
     h = lax.shift_right_logical(lax.broadcasted_iota(jnp.int32, (SSM_HEADS, HALF), 1), 6)
@@ -172,18 +182,14 @@
         some = pl.ds(g * PER_GROUP, PER_GROUP)
         return remote(dec.at[some], dsib.at[some], ex_s.at[g], ex_r.at[g], other)
 
-    def ex_half(g, half):
+    def ex_state(g):
         some = pl.ds(g * PER_GROUP, PER_GROUP)
         i = GROUPS + g
-        return remote(local.at[half, some], sib.at[half, some], ex_s.at[i], ex_r.at[i], other)
-
-    ex_rest = remote(local.at[0], sib.at[0], ex_s.at[2 * GROUPS], ex_r.at[2 * GROUPS], other)
-    first = (c == 0).astype(F32)
-
-    def link(k, i):
-        rows = pl.ds(i * CUT, CUT)
-        n = k * CUTS + i
-        return remote(isend.at[k, rows], pin.at[c, k, rows], chain_s.at[0], chain_r.at[n], above)
+        return remote(local.at[some], sib.at[some], ex_s.at[i], ex_r.at[i], other)
+
+    def link(k, half):
+        n = k * 2 + half
+        return remote(isend.at[k, half], pin.at[k, half], chain_s.at[0], chain_r.at[n], above)
 
     def own_state(g):
         for half in range(2):
@@ -196,27 +202,23 @@
             state = dot(bt[g], scaled) * last
             for i in range(PER_GROUP):
                 piece = slice(i * PIECE, (i + 1) * PIECE)
-                local[half, g * PER_GROUP + i] = state[:, piece].astype(BF16)
+                local[g * PER_GROUP + i, half] = state[:, piece].astype(BF16)
                 dec[g * PER_GROUP + i, half] = jnp.broadcast_to(last[:, piece], (8, PIECE))
 
     def chip_state(g):
         ex_d(g).wait_recv()
-        ex_half(g, c).wait_recv()
+        ex_state(g).wait_recv()
 
         def one(i, carry):
             k = g * PER_GROUP + i
-            mine, theirs = local[c, k].astype(F32), sib[c, k].astype(F32)
-            d_mine, d_theirs = dec[k, c][0:1, :], dsib[k, c][0:1, :]
-            value = first * (d_theirs * mine + theirs) + (1.0 - first) * (d_mine * theirs + mine)
-            chip[k] = value
-
-            @pl.when(y == 0)
-            def _():
-                isend[k] = value.astype(BF16)
-                for cut in range(CUTS):
-                    link(k, cut).start()
-                pin[0, k] = jnp.zeros((BLK, PIECE), BF16)
-                pin[1, k] = jnp.zeros((BLK, PIECE), BF16)
+            for half in range(2):
+                value = dec[k, half][0:1, :] * sib[k, half].astype(F32) + local[k, half].astype(F32)
+                chip[k, half] = value
+
+                @pl.when(y == 0)
+                def _(half=half, value=value):
+                    isend[k, half] = value.astype(BF16)
+                    link(k, half).start()
 
             return carry
 
@@ -224,35 +226,58 @@
 
     own_state(0)
     pl.semaphore_wait(barrier, 3)
-    ex_d(0).start()
-    ex_half(0, oc).start()
-    for e in range(KV_PARTS):
-        @pl.when(down_sends(e))
-        def _(e=e):
-            down_copy(e)[0].start()
-
-        @pl.when(up_sends(e) & (y > 0))
-        def _(e=e):
-            up_copy(e)[0].start()
+
+    @pl.when(c == 0)
+    def _():
+        ex_d(0).start()
+        ex_state(0).start()
+
+    def send_own(parts):
+        for e in parts:
+            @pl.when(down_sends(e))
+            def _(e=e):
+                down_copy(e)[0].start()
+
+            @pl.when(up_sends(e) & (y > 0))
+            def _(e=e):
+                up_copy(e)[0].start()
+
+    for i in range(2):
+        own_sib(i).start()
+
+    @pl.when(c == 0)
+    def _():
+        send_own((0, 2))
 
     for g in range(1, GROUPS):
         own_state(g)
-        ex_d(g).start()
-        ex_half(g, oc).start()
-        chip_state(g - 1)
-    chip_state(GROUPS - 1)
+
+        @pl.when(c == 0)
+        def _(g=g):
+            ex_d(g).start()
+            ex_state(g).start()
+
+        @pl.when(c == 1)
+        def _(g=g):
+            chip_state(g - 1)
+
+    @pl.when(c == 1)
+    def _():
+        chip_state(GROUPS - 1)
 
     @pl.when(y == 0)
     def _():
-        for e in range(KV_PARTS):
-            up_copy(e)[0].start()
+        pin[0 : CHUNKS - 1] = jnp.zeros((CHUNKS - 1, 2, BLK, PIECE), BF16)
+
+    @pl.when((y == 0) & (c == 1))
+    def _():
+        pin[CHUNKS - 1] = jnp.zeros((2, BLK, PIECE), BF16)
 
     @pl.when(c == 0)
     def _():
-        ex_rest.start()
-
-    for e in range(KV_PARTS):
-        kv_sib(e, me, e).start()
+        for i in range(2):
+            own_sib(i).wait_recv()
+        send_own((1, 3))
 
     for load in loads[7:]:
         load.wait()
@@ -297,17 +322,23 @@
             for i, head in enumerate(heads):
                 attn_v[:, head] = out[i * BLK : (i + 1) * BLK]
 
-    def psib(half, k):
-        return remote(pin.at[half, k], pin.at[half, k], psib_s.at[0], psib_r.at[k], other)
+    def psib(k):
+        return remote(pin.at[k], pin.at[k], psib_s.at[0], psib_r.at[k], other)
+
+    late = (y >= 2) & (y <= 4)
 
     def finish(g):
         cols = pl.ds(pl.multiple_of(g * COLS, COLS), COLS)
         state_cols = pl.ds(pl.multiple_of(g * BLK, BLK), BLK)
 
-        @pl.when(y > 0)
-        def _():
-            for i in range(PER_GROUP):
-                psib(oc, g * PER_GROUP + i).wait_recv()
+        @pl.when((y > 0) & (c == 0))
+        def _():
+            for i in range(PER_GROUP - 1):
+                psib(g * PER_GROUP + i).wait_recv()
+
+            @pl.when(jnp.logical_not(late) | (g < GROUPS - 1))
+            def _():
+                psib((g + 1) * PER_GROUP - 1).wait_recv()
 
         def part(state):
             gated = a1[:, cols] + a2[:, cols] * dot(cp[:, state_cols], state)
@@ -317,14 +348,14 @@
 
         def entering(half, i):
             k = g * PER_GROUP + i
-            came = pin[half, k].astype(F32)
-            return (dsib[k, half][0:1, :] * came + sib[half, k].astype(F32)).astype(BF16)
+            came = pin[k, half].astype(F32)
+            return (dsib[k, half][0:1, :] * came + sib[k, half].astype(F32)).astype(BF16)
 
         pieces = [(half, i) for half in range(2) for i in range(PER_GROUP)]
 
         @pl.when(c == 0)
         def _():
-            part(jnp.concatenate([pin[half, g * PER_GROUP + i] for half, i in pieces], axis=1))
+            part(jnp.concatenate([pin[g * PER_GROUP + i, half] for half, i in pieces], axis=1))
 
         @pl.when(c == 1)
         def _():
@@ -333,61 +364,70 @@
 
     reach = lax.div(y * LAG_NUM, LAG_DEN)
     attn_at = pick(y, ATTN_TICK)
+    norm_at = pick(y, NORM_TICK)
     last_chip = y == CHIPS - 1
-    drain_at = pick(y, DRAIN_TICK)
     behind = jnp.where(last_chip, CHUNKS + 2, CHUNKS + 1 + GROUPS)
-    end = jnp.maximum(jnp.maximum(reach + behind, attn_at + ATTN_PIECES), drain_at + 1)
-    late = y == 2
-    late_from = (y >= 1) & (y <= 3)
-    late_event = jnp.where(y == 1, 0, KV_PARTS)
+    end = jnp.maximum(reach + behind, attn_at + ATTN_PIECES)
+    late_from = (y >= 1) & (y <= 5)
+    late_event = jnp.where(y == 1, 0, jnp.where(y == 5, KV_PARTS + 2, KV_PARTS))
 
     def tick(t, carry):
         k = t - reach
 
-        @pl.when((y > 0) & (k >= 0) & (k < CHUNKS))
-        def _():
-            for cut in range(CUTS):
-                link(k, cut).wait_recv()
+        @pl.when((c == 1) & (y > 0) & (k >= 0) & (k < CHUNKS))
+        def _():
+            for half in range(2):
+                link(k, half).wait_recv()
 
                 @pl.when(y < CHIPS - 1)
-                def _(cut=cut):
-                    rows = slice(cut * CUT, (cut + 1) * CUT)
-                    d = dec[k, c][0:1, :] * dsib[k, c][0:1, :]
-                    isend[k, rows] = (d * pin[c, k, rows].astype(F32) + chip[k, rows]).astype(BF16)
-                    link(k, cut).start()
-
-            psib(c, k).start()
-
-        @pl.when(t < 2 * GROUPS)
-        def _():
-            own_part(t)
-
-        @pl.when(late & (k == CHUNKS))
-        def _():
+                def _(half=half):
+                    d = dec[k, half][0:1, :] * dsib[k, half][0:1, :]
+                    isend[k, half] = (d * pin[k, half].astype(F32) + chip[k, half]).astype(BF16)
+                    link(k, half).start()
+
+            psib(k).start()
+
+        @pl.when(t < GROUPS)
+        def _():
+            own_part(2 * t)
+            own_part(2 * t + 1)
+
+        @pl.when((y == 0) & (t == FIRST_TICK))
+        def _():
+            @pl.when(c == 1)
+            def _():
+                remote(isend, pin, chain_s.at[0], chain_r.at[0], above).wait_send()
+                psib(CHUNKS - 1).start()
+
+            @pl.when(c == 0)
+            def _():
+                psib(CHUNKS - 1).wait_recv()
+                for e in range(KV_PARTS):
+                    up_copy(e)[0].start()
+
+        @pl.when((c == 0) & late & (t == norm_at))
+        def _():
+            psib(CHUNKS - 1).wait_recv()
             for e in range(KV_PARTS, 2 * KV_PARTS):
-                up_copy(e)[0].start()
-
-        in_chain = last_chip & (k > PER_GROUP) & (lax.rem(k, PER_GROUP) == 1) & (k <= CHUNKS + 1)
-
-        @pl.when((c == 1) & (k == jnp.where(last_chip, PER_GROUP + 1, CHUNKS + 1)))
-        def _():
-            ex_rest.wait_recv()
-
-        @pl.when(in_chain)
-        def _():
-            finish(lax.div(k, PER_GROUP) - 1)
-
-        @pl.when(jnp.logical_not(last_chip) & (k == CHUNKS + 1))
-        def _():
-            for g in range(GROUPS):
+                @pl.when((y < 4) | (e >= KV_PARTS + 2))
+                def _(e=e):
+                    up_copy(e)[0].start()
+
+        @pl.when(t == norm_at)
+        def _():
+            for g in range(GROUPS - 1):
                 finish(g)
 
-        e = lax.div(t, KV_TICKS) - 1
-        now = (lax.rem(t, KV_TICKS) == 0) & (e >= 0)
+        @pl.when(t == jnp.where(last_chip, reach + CHUNKS + 1, norm_at))
+        def _():
+            finish(GROUPS - 1)
+
+        e = lax.div(t - KV_FIRST + KV_TICKS, KV_TICKS) - 1
+        now = (c == 0) & (lax.rem(t, KV_TICKS) == 0) & (t >= KV_FIRST)
 
         @pl.when(now & (e < KV_PARTS * DOWN_STEPS) & down_gets(jnp.maximum(e, 0)))
         def _():
-            arrival, slot, part = down_copy(e, 1)
+            arrival, piece = down_copy(e, 1)
             arrival.wait_recv()
 
             @pl.when((e < KV_PARTS * (DOWN_STEPS - 1)) & down_sends(e + KV_PARTS))
@@ -396,56 +436,28 @@
 
             @pl.when(down_keeps(e))
             def _():
-                kv_sib(DOWN0 + e, slot, part).start()
-
-        behind = late_from & (k > CHUNKS) & (k <= CHUNKS + KV_PARTS)
-        u = jnp.where(behind, k - CHUNKS - 1 + late_event, e)
+                kv_sib(DOWN0 + e, piece).start()
+
+        behind = (c == 0) & late_from & (k > CHUNKS + LATE) & (k <= CHUNKS + LATE + KV_PARTS)
+        u = jnp.where(behind, k - CHUNKS - LATE - 1 + late_event, e)
         due = behind | (now & (e < KV_PARTS * UP_STEPS) & (jnp.logical_not(late_from) | (e < late_event)))
 
         @pl.when(due & up_gets(jnp.maximum(u, 0)))
         def _():
-            arrival, slot, part = up_copy(u, 1)
+            arrival, piece = up_copy(u, 1)
             arrival.wait_recv()
 
-            @pl.when((u < KV_PARTS * (UP_STEPS - 1)) & up_sends(u + KV_PARTS) & jnp.logical_not(late))
+            @pl.when((u < KV_PARTS * (UP_STEPS - 1)) & up_sends(u + KV_PARTS) & (jnp.logical_not(late) | ((y == 4) & (u < 2))))
             def _():
                 up_copy(u + KV_PARTS)[0].start()
 
-            kv_sib(UP0 + u, slot, part).start()
-
-        @pl.when(t == attn_at)
-        def _():
-            for i in range(KV_PARTS):
-                kv_sib(i, me, 0).wait_recv()
-
-            def wait_up(i, carry):
-                @pl.when(up_gets(i))
-                def _():
-                    kv_sib(UP0 + i, me, 0).wait_recv()
-                return carry
-
-            def wait_down(i, carry):
-                @pl.when(down_keeps(i))
-                def _():
-                    kv_sib(DOWN0 + i, me, 0).wait_recv()
-                return carry
-
-            lax.fori_loop(0, KV_PARTS * UP_STEPS, wait_up, 0)
-            lax.fori_loop(0, KV_PARTS * DOWN_STEPS, wait_down, 0)
-
-        @pl.when((t >= attn_at) & (t < attn_at + ATTN_PIECES))
-        def _():
-            attention(t - attn_at)
-
-        @pl.when(t == drain_at)
-        def _():
-            @pl.when(c == 0)
-            def _():
-                ex_rest.wait_send()
-
+            kv_sib(UP0 + u, piece).start()
+
+        @pl.when((t == attn_at) & (c == 0))
+        def _():
             for g in range(GROUPS):
                 ex_d(g).wait_send()
-                ex_half(g, oc).wait_send()
+                ex_state(g).wait_send()
 
             def wait_up_sent(i, carry):
                 @pl.when(up_sends(i))
@@ -454,7 +466,7 @@
 
                 @pl.when(up_gets(i))
                 def _():
-                    kv_sib(UP0 + i, me, 0).wait_send()
+                    kv_sib(UP0 + i, kv.at[me, 0]).wait_send()
                 return carry
 
             def wait_down_sent(i, carry):
@@ -464,25 +476,53 @@
 
                 @pl.when(down_keeps(i))
                 def _():
-                    kv_sib(DOWN0 + i, me, 0).wait_send()
+                    kv_sib(DOWN0 + i, kv.at[me, 0]).wait_send()
                 return carry
 
             lax.fori_loop(0, KV_PARTS * UP_STEPS, wait_up_sent, 0)
             lax.fori_loop(0, KV_PARTS * DOWN_STEPS, wait_down_sent, 0)
-            for i in range(KV_PARTS):
-                kv_sib(i, me, i).wait_send()
+            for i in range(2):
+                own_sib(i).wait_send()
+
+        @pl.when((t == attn_at) & (c == 1))
+        def _():
+            for i in range(2):
+                own_sib(i).wait()
+
+            def wait_up(i, carry):
+                @pl.when(up_gets(i))
+                def _():
+                    kv_sib(UP0 + i, kv.at[me, 0]).wait_recv()
+                return carry
+
+            def wait_down(i, carry):
+                @pl.when(down_keeps(i))
+                def _():
+                    kv_sib(DOWN0 + i, kv.at[me, 0]).wait_recv()
+                return carry
+
+            lax.fori_loop(0, KV_PARTS * UP_STEPS, wait_up, 0)
+            lax.fori_loop(0, KV_PARTS * DOWN_STEPS, wait_down, 0)
+
+        @pl.when((t >= attn_at) & (t < attn_at + ATTN_PIECES))
+        def _():
+            attention(t - attn_at)
 
         return carry
 
     lax.fori_loop(0, end, tick, 0)
 
-    @pl.when(y > 0)
-    def _():
-        remote(pin.at[c], pin.at[c], psib_s.at[0], psib_r.at[0], other).wait_send()
-
-    @pl.when(y < CHIPS - 1)
-    def _():
-        remote(isend, pin.at[c], chain_s.at[0], chain_r.at[0], above).wait_send()
+    @pl.when((y > 0) & (c == 1))
+    def _():
+        remote(pin, pin, psib_s.at[0], psib_r.at[0], other).wait_send()
+
+    @pl.when((y > 0) & (y < CHIPS - 1) & (c == 1))
+    def _():
+        remote(isend, pin, chain_s.at[0], chain_r.at[0], above).wait_send()
+
+    @pl.when((y == 0) & (c == 1))
+    def _():
+        psib(CHUNKS - 1).wait_send()
 
 
 def store_kernel(ssm, attn, ssm_out, attn_out, sem):
@@ -519,15 +559,15 @@
             vmem((2 * BLK + 64, SSM_HEADS), BF16), vmem((2 * GROUPS, SSM_HEADS, HALF), BF16),
             vmem((GROUPS, BLK, BLK), BF16),
             vmem((BLK, wide), BF16), vmem((BLK, wide), F32), vmem((BLK, wide), F32),
-            vmem((2, CHUNKS, BLK, PIECE), BF16), vmem((2, CHUNKS, BLK, PIECE), BF16),
+            vmem((CHUNKS, 2, BLK, PIECE), BF16), vmem((CHUNKS, 2, BLK, PIECE), BF16),
             vmem((CHUNKS, 2, 8, PIECE), F32), vmem((CHUNKS, 2, 8, PIECE), F32),
-            vmem((CHUNKS, BLK, PIECE), F32), vmem((CHUNKS, BLK, PIECE), BF16),
-            vmem((2, CHUNKS, BLK, PIECE), BF16),
+            vmem((CHUNKS, 2, BLK, PIECE), F32), vmem((CHUNKS, 2, BLK, PIECE), BF16),
+            vmem((CHUNKS, 2, BLK, PIECE), BF16),
             dma(12),
             dma(KV_PARTS * UP_STEPS), dma(KV_PARTS * UP_STEPS), dma(KV_PARTS * DOWN_STEPS),
-            dma(KV_PARTS * DOWN_STEPS), dma(KV_PARTS * (1 + UP_STEPS + DOWN_STEPS)),
-            dma(KV_PARTS * (1 + UP_STEPS + DOWN_STEPS)),
-            dma(1), dma(CHUNKS * CUTS), dma(1), dma(CHUNKS), dma(2 * GROUPS + 1), dma(2 * GROUPS + 1),
+            dma(KV_PARTS * DOWN_STEPS), dma(2 + KV_PARTS * (UP_STEPS + DOWN_STEPS)),
+            dma(2 + KV_PARTS * (UP_STEPS + DOWN_STEPS)),
+            dma(1), dma(2 * CHUNKS), dma(1), dma(CHUNKS), dma(2 * GROUPS), dma(2 * GROUPS),
         ],
         compiler_params=pltpu.CompilerParams(
             collective_id=0, has_side_effects=True, vmem_limit_bytes=60 * 2**20

time: 45.6 us -> 44 us (0.965); the launches traced: 45.4 us -> 43.3 us
  Pallas kernels: 44.8 us -> 42.7 us
    pallas_call x1, Pallas kernels: 43.6 us -> 41.5 us  [body(): pl.pallas_call(kernel, out_shape=(vmem((BLK, wide), BF16), vmem((BLK, hea...]
where the time goes in v5:
time: 44 us; the launch traced here: 43.3 us
  Pallas kernels  42.7 us (97%)
  between operations  0.64 us (1%)
    pallas_call x1, Pallas kernels, body(): pl.pallas_call(kernel, out_shape=(vmem((BLK, wide), BF16), vmem((BLK, hea...  41.5 us
    pallas_call x1, Pallas kernels, body(): pl.pallas_call(store_kernel, out_shape=outs, in_specs=[vmem_spec] * 2, ou...  1.17 us

profile of v5, /device:TPU:48, one launch (start us, length us, event | category | flops | bytes accessed | tf_op | source)
XLA Modules:
  0.0 43.3 jit_solution(354903394715972720)
XLA Ops:
  0.6 41.5 %layers.1 = (bf16[128,4096]{1,0:T(8,128)(2,1)S(1)}, bf16[128,2048]{1,0:T(8,128)(2,1)S(1)}) custom-call(bf16[128,4096]{1,0:T(8,128)(2,1)} %x_hbm.1, bf16[128,4096]{1,0:T(8,128)(2,1)} %gate_hbm.1, bf16[128,512]{1,0:T(8,128)(2,1)} %b_hbm.1, bf16[128,512]{1,0:T(8,128)(2,1)} %c_hbm.1, f32[64,128]{1,0:T(8,128)} %bitcast.4, f32[1,64]{1,0:T(1,128)} %bitcast.6, ...), custom_call_target="tpu_custom_call" | custom-call | tf_op jit(solution)/shard_map/layers/pallas_call | solution.py:548
  42.1 1.2 %store.1 = (bf16[128,4096]{1,0:T(8,128)(2,1)}, bf16[128,2048]{1,0:T(8,128)(2,1)}) custom-call(bf16[128,4096]{1,0:T(8,128)(2,1)S(1)} %get-tuple-element.4.ssm, bf16[128,2048]{1,0:T(8,128)(2,1)S(1)} %get-tuple-element.5.attn), custom_call_target="tpu_custom_call" | custom-call | tf_op jit(solution)/shard_map/store/pallas_call | solution.py:580

commit v6 on v5

--- a/solution.py
+++ b/solution.py
@@ -28,13 +28,13 @@
 CHUNKS = GROUPS * PER_GROUP
 UP_STEPS = 3
 DOWN_STEPS = 5
-LAG_NUM, LAG_DEN = 10, 3
+LAG_NUM, LAG_DEN = 7, 2
 KV_PARTS = 4
 KV_TICKS = 2
 KV_FIRST = 4
 LATE = 4
 FIRST_TICK = 22
-NORM_TICK = (23, 23, 22, 26, 33, 38, 37, 35)
+NORM_TICK = (23, 23, 23, 26, 34, 38, 37, 35)
 ATTN_TICK = (32, 28, 31, 43, 43, 43, 43, 39)
 ATTN_KEY_HEADS = 4
 STORES = 2
@@ -65,7 +65,7 @@
     x_hbm, gate_hbm, b_hbm, c_hbm, dt_hbm, alog_hbm, skip_hbm, gain_hbm, q_hbm, k_hbm, v_hbm, list_hbm,
     ssm_v, attn_v,
     x, gate, b, cp, dtr, alog, skip, gain, q, lists,
-    kv, stack, spread, bt, xs, a1, a2, local, sib, dec, dsib, chip, isend, pin,
+    kv, stack, spread, xs, a1, a2, local, sib, dec, dsib, chip, isend, pin,
     in_sem,
     up_s, up_r, down_s, down_r, kvsib_s, kvsib_r, chain_s, chain_r, psib_s, psib_r, ex_s, ex_r,
 ):
@@ -173,8 +173,6 @@
     stack[BLK + 32 : 2 * BLK + 32, :] = up_to.astype(BF16)
     stack[2 * BLK + 32 : 2 * BLK + 48, :] = s_hi
     stack[2 * BLK + 48 : 2 * BLK + 64, :] = s_lo
-    for g in range(GROUPS):
-        bt[g] = jnp.transpose(b[:, g * BLK : (g + 1) * BLK].astype(F32)).astype(BF16)
     for load in loads[4:7]:
         load.wait()
 
@@ -192,6 +190,7 @@
         return remote(isend.at[k, half], pin.at[k, half], chain_s.at[0], chain_r.at[n], above)
 
     def own_state(g):
+        bt = jnp.transpose(b[:, g * BLK : (g + 1) * BLK].astype(F32)).astype(BF16)
         for half in range(2):
             j = 2 * g + half
             cols = pl.ds(j * HALF, HALF)
@@ -199,7 +198,7 @@
             scaled = (x[:, cols].astype(F32) * wide[0:BLK]).astype(BF16)
             xs[:, cols] = scaled
             last = wide[BLK : BLK + 1] + wide[BLK + 16 : BLK + 17]
-            state = dot(bt[g], scaled) * last
+            state = dot(bt, scaled) * last
             for i in range(PER_GROUP):
                 piece = slice(i * PIECE, (i + 1) * PIECE)
                 local[g * PER_GROUP + i, half] = state[:, piece].astype(BF16)
@@ -261,6 +260,13 @@
         def _(g=g):
             chip_state(g - 1)
 
+        if g == 2:
+            @pl.when(c == 0)
+            def _():
+                for i in range(2):
+                    own_sib(i).wait_recv()
+                send_own((1, 3))
+
     @pl.when(c == 1)
     def _():
         chip_state(GROUPS - 1)
@@ -273,11 +279,6 @@
     def _():
         pin[CHUNKS - 1] = jnp.zeros((2, BLK, PIECE), BF16)
 
-    @pl.when(c == 0)
-    def _():
-        for i in range(2):
-            own_sib(i).wait_recv()
-        send_own((1, 3))
 
     for load in loads[7:]:
         load.wait()
@@ -557,7 +558,6 @@
             pltpu.SMEM((1, 3), jnp.int32),
             vmem((2 * CHIPS, 2, BLK, KVHEADS * HEAD_D), BF16),
             vmem((2 * BLK + 64, SSM_HEADS), BF16), vmem((2 * GROUPS, SSM_HEADS, HALF), BF16),
-            vmem((GROUPS, BLK, BLK), BF16),
             vmem((BLK, wide), BF16), vmem((BLK, wide), F32), vmem((BLK, wide), F32),
             vmem((CHUNKS, 2, BLK, PIECE), BF16), vmem((CHUNKS, 2, BLK, PIECE), BF16),
             vmem((CHUNKS, 2, 8, PIECE), F32), vmem((CHUNKS, 2, 8, PIECE), F32),

time: 44 us -> 44 us (level)
  no operation moved by 1% of the time
where the time goes in v6:
time: 44 us; the launch traced here: 43.3 us
  Pallas kernels  42.7 us (97%)
  between operations  0.64 us (1%)
    pallas_call x1, Pallas kernels, body(): pl.pallas_call(kernel, out_shape=(vmem((BLK, wide), BF16), vmem((BLK, hea...  41.5 us
    pallas_call x1, Pallas kernels, body(): pl.pallas_call(store_kernel, out_shape=outs, in_specs=[vmem_spec] * 2, ou...  1.17 us

profile of v6, /device:TPU:48, one launch (start us, length us, event | category | flops | bytes accessed | tf_op | source)
XLA Modules:
  0.0 43.3 jit_solution(3084127680539330933)
XLA Ops:
  0.6 41.5 %layers.1 = (bf16[128,4096]{1,0:T(8,128)(2,1)S(1)}, bf16[128,2048]{1,0:T(8,128)(2,1)S(1)}) custom-call(bf16[128,4096]{1,0:T(8,128)(2,1)} %x_hbm.1, bf16[128,4096]{1,0:T(8,128)(2,1)} %gate_hbm.1, bf16[128,512]{1,0:T(8,128)(2,1)} %b_hbm.1, bf16[128,512]{1,0:T(8,128)(2,1)} %c_hbm.1, f32[64,128]{1,0:T(8,128)} %bitcast.4, f32[1,64]{1,0:T(1,128)} %bitcast.6, ...), custom_call_target="tpu_custom_call" | custom-call | tf_op jit(solution)/shard_map/layers/pallas_call | solution.py:549
  42.1 1.2 %store.1 = (bf16[128,4096]{1,0:T(8,128)(2,1)}, bf16[128,2048]{1,0:T(8,128)(2,1)}) custom-call(bf16[128,4096]{1,0:T(8,128)(2,1)S(1)} %get-tuple-element.4.ssm, bf16[128,2048]{1,0:T(8,128)(2,1)S(1)} %get-tuple-element.5.attn), custom_call_target="tpu_custom_call" | custom-call | tf_op jit(solution)/shard_map/store/pallas_call | solution.py:580
